TPU v7x, 512 devices: a whole 4x8x8 slice. The times are simulated.
512 devices in a mesh: dp: 64 (over x, z, y_lo), tensor: 8 (over y_hi, core).
Axes of the slice: x: 4, y: 8 (y_hi: 4, y_lo: 2; y = y_hi * 2 + y_lo), z: 8, core: 2. Of those that a mesh axis runs over, the one named last changes fastest.
Arguments:
- acts: bfloat16 [16384, 1024], P('dp'), may hold values from -8 to 8
- up_grad: bfloat16 [16384, 8192], P('dp', 'tensor'), may hold values from -8 to 8
Outputs:
- left_root: float32 [1024, 8192], P('dp', 'tensor')
- right_root: float32 [1024, 8192], P('dp', 'tensor')
- update: float32 [1024, 8192], P('dp', 'tensor')
All inputs are finite; a program needn't handle non-finite values.
Results may differ from a plain program's by a relative error of at most 0.0011.
The roundings to bfloat16 on the way count: a program that leaves them out, or rounds other values in their place, can miss the bound.
Values may be sent and summed in bfloat16 or wider, within the bound.
No kernel may reach another device: no remote copies, remote signals or barrier semaphores. Data moves between devices by JAX's collectives and lax.ppermute only.
A program may use at most 64 MiB of HBM per device.

v0:
```python
import jax
import jax.numpy as jnp
from jax import lax
from jax.sharding import PartitionSpec as P

NEWTON = 2


DAMPING = 1e-06


def make_step(apply_power):

    def stepped(vector):
        return (5.0 * vector - apply_power(vector)) * 0.25

    return stepped


def make_dense(matrix):

    def dense(vector):
        return jnp.dot(vector, matrix, precision=lax.Precision.HIGHEST)

    return dense


def make_left(grad_wide, scale):

    def left_apply(vector):
        inner = jnp.dot(vector, grad_wide, precision=lax.Precision.HIGHEST)
        outer = lax.dot_general(
            inner, grad_wide, (((1,), (1,)), ((), ())), precision=lax.Precision.HIGHEST
        )
        return (outer + DAMPING * vector) / scale

    return left_apply


def make_right(grad_wide, scale):

    def right_apply(vector):
        inner = lax.dot_general(
            vector, grad_wide, (((1,), (1,)), ((), ())), precision=lax.Precision.HIGHEST
        )
        outer = jnp.dot(inner, grad_wide, precision=lax.Precision.HIGHEST)
        return (outer + DAMPING * vector) / scale

    return right_apply


def per_device(acts, up_grad):
    owners = lax.axis_size("dp")
    blocks = lax.axis_size("tensor")
    width = acts.shape[1]
    rows = width // owners
    tokens_all = acts.shape[0] * owners
    start = lax.axis_index("dp") * rows
    summed = lax.dot_general(
        acts, up_grad, (((0,), (0,)), ((), ())), preferred_element_type=jnp.float32
    )
    grad_rows = lax.psum_scatter(summed / tokens_all, "dp", scatter_dimension=0, tiled=True)
    grad_low = grad_rows.astype(jnp.bfloat16)
    grad_full = lax.all_gather(grad_low, "dp", axis=0, tiled=True)
    grad_wide = grad_full.astype(jnp.float32)
    col_index = lax.broadcasted_iota(jnp.int32, (rows, width), 1)
    row_index = lax.broadcasted_iota(jnp.int32, (rows, width), 0)
    eye_rows = (col_index == start + row_index).astype(jnp.float32)
    left_rows = (
        lax.dot_general(
            grad_low, grad_full, (((1,), (1,)), ((), ())), preferred_element_type=jnp.float32
        )
        + DAMPING * eye_rows
    )
    col_slab = lax.dynamic_slice_in_dim(grad_full, start, rows, 1)
    right_rows = (
        lax.dot_general(
            col_slab, grad_full, (((0,), (0,)), ((), ())), preferred_element_type=jnp.float32
        )
        + DAMPING * eye_rows
    )
    scale = jnp.sqrt(lax.psum(jnp.sum(left_rows * left_rows), "dp"))
    apply_left = make_left(grad_wide, scale)
    apply_right = make_right(grad_wide, scale)
    left_power = left_rows / scale
    right_power = right_rows / scale
    left_root = eye_rows
    right_root = eye_rows
    right_steps = []
    for step in range(NEWTON):
        left_step = make_step(apply_left)
        right_step = make_step(apply_right)
        right_steps.append(right_step)
        left_root = left_step(left_root)
        right_root = right_step(right_root)
        if step + 1 < NEWTON:
            for power in range(4):
                left_power = left_step(left_power)
                right_power = right_step(right_power)
            left_full, right_full = (
                lax.all_gather(left_power.astype(jnp.bfloat16), "dp", axis=0, tiled=True).astype(
                    left_power.dtype
                ),
                lax.all_gather(right_power.astype(jnp.bfloat16), "dp", axis=0, tiled=True).astype(
                    right_power.dtype
                ),
            )
            apply_left = make_dense(left_full)
            apply_right = make_dense(right_full)
    product = jnp.dot(left_root, grad_wide, precision=lax.Precision.HIGHEST)
    for right_step in right_steps:
        product = right_step(product)
    total = lax.psum(jnp.sum(product * product), ("dp", "tensor"))
    count = width * width * blocks
    update = product * lax.rsqrt(total / count + 1e-06)
    return (left_root, right_root, update)


def solution(mesh):
    return jax.shard_map(
        per_device,
        mesh=mesh,
        in_specs=(P("dp", None), P("dp", "tensor")),
        out_specs=(P("dp", "tensor"), P("dp", "tensor"), P("dp", "tensor")),
        check_vma=False,
    )
```

profile of v0, /device:TPU:1, one launch (start us, length us, event | category | flops | bytes accessed | tf_op | source)
XLA Modules:
  0.0 1529.0 jit_solution(15832953756083793230)
XLA Ops:
  7.2 1.0 copy-done
  8.2 3.7 convolution_multiply_fusion
  12.0 287.7 %reduce-scatter.2.cloned.1.call-done = f32[16,1024]{1,0:T(8,128)} async-done(((f32[1024,1024]{1,0:T(8,128)}), f32[16,1024]{1,0:T(8,128)}) %reduce-scatter.2.cloned.1.call-update) | async-done | bytes 65552 | tf_op jit(solution)/shard_map/reduce_scatter | solution.py:62
  299.7 1.5 convert_element_type.6
  301.2 301.2 %all-gather.4.cloned.1.call-done = bf16[1024,1024]{1,0:T(8,128)(2,1)} async-done(((bf16[16,1024]{1,0:T(8,128)(2,1)}), bf16[1024,1024]{1,0:T(8,128)(2,1)}) %all-gather.4.cloned.1.call-update) | async-done | bytes 2097168 | tf_op jit(solution)/shard_map/all_gather | solution.py:64
  602.5 3.0 multiply_reduce_fusion.1
  605.5 131.5 %psum.14 = f32[]{:T(128)} all-reduce(f32[]{:T(128)} %get-tuple-element.3), channel_id=1, replica_groups=mesh['dp'=64,'tensor'=8] {'dp'}, use_global_device_ids=true, to_apply=%region_2.0 | all-reduce | flops 1 | bytes 8 | tf_op jit(solution)/shard_map/psum | solution.py:82
  738.7 1.7 fusion.24
  740.4 0.9 fusion.42
  741.4 1.7 fusion.22
  743.1 0.9 fusion.40
  744.0 1.7 fusion.20
  745.8 0.9 fusion.38
  746.7 2.4 fusion.27
  749.9 1.7 fusion.69
  751.6 0.9 fusion.11
  752.6 1.7 fusion.35
  754.3 0.9 fusion.9
  755.2 1.7 fusion.33
  757.0 0.9 fusion.7
  757.9 1.7 fusion.31
  759.7 1.6 fusion.28
  762.3 1.7 fusion.26
  764.1 0.9 fusion.14
  765.0 309.0 %all-gather.6.cloned.1.call-done = bf16[1024,1024]{1,0:T(8,128)(2,1)} async-done(((bf16[16,1024]{1,0:T(8,128)(2,1)}), bf16[1024,1024]{1,0:T(8,128)(2,1)}) %all-gather.6.cloned.1.call-update) | async-done | bytes 2097168 | tf_op jit(solution)/shard_map/all_gather | solution.py:101
  1074.0 2.5 fusion.15
  1077.5 1.9 fusion.71
  1079.4 0.9 fusion.1
  1080.4 295.9 %all-gather.8.cloned.1.call-done = bf16[1024,1024]{1,0:T(8,128)(2,1)} async-done(((bf16[16,1024]{1,0:T(8,128)(2,1)}), bf16[1024,1024]{1,0:T(8,128)(2,1)}) %all-gather.8.cloned.1.call-update) | async-done | bytes 2097168 | tf_op jit(solution)/shard_map/all_gather | solution.py:104
  1376.2 3.3 multiply_reduce_fusion
  1379.5 140.0 %psum.15 = f32[]{:T(128)} all-reduce(f32[]{:T(128)} %get-tuple-element.5), channel_id=1, replica_groups=mesh['dp'=64,'tensor'=8] {'dp','tensor'}, use_global_device_ids=true, to_apply=%region_4.0 | all-reduce | flops 1 | bytes 8 | tf_op jit(solution)/shard_map/psum | solution.py:113
  1520.9 1.6 fusion.2
  (22 shorter events, 4.5 us)
Async XLA Ops:
  7.2 1.0 copy-start
  7.2 292.5 %reduce-scatter.2.cloned.1.call-start = ((), (), s32[]{:S(2)}) async-start(), calls=%async_computation.1 | async-start | bytes 4259840 | tf_op jit(solution)/shard_map/reduce_scatter | solution.py:62
  12.0 590.5 %all-gather.4.cloned.1.call-start = ((), (), s32[]{:S(2)}) async-start(), calls=%async_computation.2 | async-start | bytes 2129920 | tf_op jit(solution)/shard_map/all_gather | solution.py:64
  301.2 772.8 %all-gather.6.cloned.1.call-start = ((), (), s32[]{:S(2)}) async-start(), calls=%async_computation.3 | async-start | bytes 2129920 | tf_op jit(solution)/shard_map/all_gather | solution.py:101
  602.5 135.3 %copy-start.1 = (bf16[1024,1024]{1,0:T(8,128)(2,1)S(1)}, bf16[1024,1024]{1,0:T(8,128)(2,1)}, u32[]{:S(2)}) copy-start(bf16[1024,1024]{1,0:T(8,128)(2,1)} %all-gather.4.cloned.1.call-done) | copy-start | bytes 6291460
  749.1 627.1 %all-gather.8.cloned.1.call-start = ((), (), s32[]{:S(2)}) async-start(), calls=%async_computation.4 | async-start | bytes 2129920 | tf_op jit(solution)/shard_map/all_gather | solution.py:104
  1076.5 2.9 copy-start.3
  1376.2 144.6 %copy-start.2 = (bf16[1024,1024]{1,0:T(8,128)(2,1)S(1)}, bf16[1024,1024]{1,0:T(8,128)(2,1)}, u32[]{:S(2)}) copy-start(bf16[1024,1024]{1,0:T(8,128)(2,1)} %all-gather.8.cloned.1.call-done) | copy-start | bytes 6291460
Sparse Core Ops, SparseCore 0:
  12.1 287.5 reduce-scatter.1
  302.6 299.8 all-gather.3
  749.2 324.7 all-gather.5
  1076.7 299.4 all-gather.7
where the time goes:
time: 1530 us
  waiting for transfers between devices  1190 us (78%)
  blocking collectives  272 us (18%)
  matrix products  44.9 us (3%)
    all_gather x1, waiting for transfers between devices, per_device(): lax.all_gather(left_power.astype(jnp.bfloat16), 'dp', axis=0, tiled=True)  309 us
    all_gather x1, waiting for transfers between devices, per_device(): grad_full = lax.all_gather(grad_low, 'dp', axis=0, tiled=True)  301 us
    all_gather x1, waiting for transfers between devices, per_device(): lax.all_gather(right_power.astype(jnp.bfloat16), 'dp', axis=0, tiled=True)  296 us
    reduce_scatter x1, waiting for transfers between devices, per_device(): lax.psum_scatter(summed / tokens_all, 'dp', scatter_dimension=0, tiled=True)  288 us
    psum x1, blocking collectives, per_device(): total = lax.psum(jnp.sum(product * product), ('dp', 'tensor'))  140 us
    psum x1, blocking collectives, per_device(): scale = jnp.sqrt(lax.psum(jnp.sum(left_rows * left_rows), 'dp'))  132 us
  transfers between devices with their start and end apart: 4, of which 4 were waited for; matrix products, arithmetic and copies ran while one was open for 1% of the time, Pallas kernels for 0%

commit v1 on v0

v1 whole, which is shorter than its diff:
```python
import jax
import jax.numpy as jnp
from jax import lax
from jax.experimental import pallas as pl
from jax.experimental.pallas import tpu as pltpu
from jax.sharding import Mesh, PartitionSpec as P

DAMPING = 1e-06
SIZES = (4, 8, 2, 4, 2)
NAMES = ("x", "z", "yl", "yh", "core")
DP = ("x", "z", "yl")
TENSOR = ("yh", "core")
PLANE = ("x", "yl")
F32 = jnp.float32
LOW = jnp.bfloat16


def times(vector, weight):
    rows = vector.shape[0]
    high = vector.astype(LOW)
    rest = (vector - high.astype(F32)).astype(LOW)
    both = jnp.dot(
        jnp.concatenate([high, rest], axis=0), weight, preferred_element_type=F32
    )
    return both[:rows] + both[rows:]


def roots_kernel(start_ref, tiles_ref, left_ref, right_ref, product_ref, total_ref, grad, flip):
    width = grad.shape[0]
    rows = left_ref.shape[0]
    n_tiles, high, wide = tiles_ref.shape
    start = pl.multiple_of(start_ref[0], rows)
    for index in range(n_tiles):
        col, row = index // 2, index % 2
        grad[row * high : (row + 1) * high, col * wide : (col + 1) * wide] = tiles_ref[index]
    for row in range(0, width, 256):
        for col in range(0, width, 256):
            flip[col : col + 256, row : row + 256] = grad[
                row : row + 256, col : col + 256
            ].T
    total = jnp.zeros((256, 256), F32)
    trace = jnp.zeros((256, width), F32)
    for row in range(0, width, 256):
        part = grad[row : row + 256, :]
        wide_part = part.astype(F32)
        trace += wide_part * wide_part
        for col in range(row, width, 256):
            stat = jnp.dot(part, flip[:, col : col + 256], preferred_element_type=F32)
            total += (1.0 if col == row else 2.0) * (stat * stat)
    square = jnp.sum(total) + 2.0 * DAMPING * jnp.sum(trace) + width * DAMPING * DAMPING
    inverse = lax.rsqrt(jnp.full((1, 1), square, F32))

    col_index = lax.broadcasted_iota(jnp.int32, (rows, width), 1)
    row_index = lax.broadcasted_iota(jnp.int32, (rows, width), 0)
    eye = (col_index == start + row_index).astype(F32)

    def finish(vector, outer):
        return (outer + DAMPING * vector) * inverse

    def stepped(vector, power):
        return (5.0 * vector - power) * 0.25

    def left_power(vector):
        return finish(vector, times(times(vector, grad[...]), flip[...]))

    first = jnp.dot(grad[pl.ds(start, rows), :], flip[...], preferred_element_type=F32)
    root = stepped(eye, finish(eye, first))
    vector = root
    for _ in range(4):
        vector = stepped(vector, left_power(vector))
    left = stepped(root, left_power(vector))
    left_ref[...] = left

    high_left = left.astype(LOW)
    rest_left = (left - high_left.astype(F32)).astype(LOW)
    both = jnp.dot(
        jnp.concatenate([high_left, rest_left, flip[pl.ds(start, rows), :]], axis=0),
        grad[...],
        preferred_element_type=F32,
    )
    product = both[:rows] + both[rows : 2 * rows]
    right = stepped(eye, finish(eye, both[2 * rows :]))

    def right_power(vector):
        return finish(vector, times(times(vector, flip[...]), grad[...]))

    product = stepped(product, right_power(product))
    root = jnp.concatenate([right, product], axis=0)
    vector = root
    for _ in range(4):
        vector = stepped(vector, right_power(vector))
    root = stepped(root, right_power(vector))
    right_ref[...] = root[:rows]
    product = root[rows:]
    product_ref[...] = product
    total_ref[...] = jnp.full(total_ref.shape, jnp.sum(product * product), F32)


def roots(start, tiles, rows, devices):
    width = 1024
    shape = jax.ShapeDtypeStruct((rows, width), F32)
    vmem = pl.BlockSpec(memory_space=pltpu.VMEM)
    return pl.pallas_call(
        roots_kernel,
        out_shape=(shape, shape, shape, jax.ShapeDtypeStruct((devices, 128), F32)),
        in_specs=[pl.BlockSpec(memory_space=pltpu.SMEM), vmem],
        out_specs=(vmem, vmem, vmem, vmem),
        scratch_shapes=[pltpu.VMEM((width, width), LOW), pltpu.VMEM((width, width), LOW)],
        compiler_params=pltpu.CompilerParams(vmem_limit_bytes=32 * 1024 * 1024),
    )(start, tiles)


def pack_kernel(core_ref, acts_ref, grad_ref, sent_ref):
    core = core_ref[0]
    for index in range(sent_ref.shape[0]):
        col, row = index // 2, index % 2
        begin = pl.multiple_of(row * 512 + core * 256, 256)
        sent_ref[index, :, :256] = acts_ref[:, pl.ds(begin, 256)]
        sent_ref[index, :, 256:] = grad_ref[:, col * 256 : (col + 1) * 256]


def pack(core, acts, up_grad, plane):
    vmem = pl.BlockSpec(memory_space=pltpu.VMEM)
    return pl.pallas_call(
        pack_kernel,
        out_shape=jax.ShapeDtypeStruct((plane, acts.shape[0], 512), LOW),
        in_specs=[pl.BlockSpec(memory_space=pltpu.SMEM), vmem, vmem],
        out_specs=vmem,
        compiler_params=pltpu.CompilerParams(vmem_limit_bytes=16 * 1024 * 1024),
    )(core.astype(jnp.int32).reshape(1), acts, up_grad)


def against(left, right):
    return lax.dot_general(left, right, (((0,), (0,)), ((), ())), preferred_element_type=F32)


def per_device(acts, up_grad):
    tokens, width = acts.shape
    owners = 64
    rows = width // owners
    plane = 8
    depth = 8
    core = lax.axis_index("core")
    sent = pack(core, acts, up_grad, plane)
    got = lax.all_to_all(sent, PLANE, 0, 0, tiled=True).reshape(plane * tokens, 512)
    mine, cols = got[:, :256], got[:, 256:]
    other = lax.ppermute(mine, "core", [(0, 1), (1, 0)])
    mine, other = against(mine, cols), against(other, cols)
    tile = jnp.where(
        core == 0, jnp.concatenate([mine, other]), jnp.concatenate([other, mine])
    ).reshape(depth, 64, 256)
    parts = lax.all_to_all(tile, "z", 0, 0, tiled=True)
    piece = (jnp.sum(parts, axis=0) / (tokens * owners)).astype(LOW)
    tile = lax.all_to_all(jnp.broadcast_to(piece[None], (depth, 64, 256)), "z", 0, 0, tiled=True)
    tile = tile.reshape(512, 256)
    tiles = lax.all_to_all(
        jnp.broadcast_to(tile[None], (plane, 512, 256)), PLANE, 0, 0, tiled=True
    )
    start = (lax.axis_index(DP) * rows).astype(jnp.int32).reshape(1)
    left, right, product, total = roots(start, tiles, rows, 512)
    totals = lax.all_to_all(total, DP + TENSOR, 0, 0, tiled=True)
    mean = jnp.sum(totals[:, 0]) / (width * width * 8)
    update = product * lax.rsqrt(mean + 1e-06)
    return (left, right, update)


def solution(mesh):
    fine = Mesh(mesh.devices.reshape(SIZES), NAMES)
    out = P(DP, TENSOR)
    return jax.shard_map(
        per_device,
        mesh=fine,
        in_specs=(P(DP, None), P(DP, TENSOR)),
        out_specs=(out, out, out),
        check_vma=False,
    )
```

time: 1530 us -> 156 us (0.10)
  waiting for transfers between devices: 1190 us -> 25.7 us
  blocking collectives: 272 us -> 99.9 us
  matrix products: 44.9 us -> 0.94 us
    all_gather x3 -> x0, waiting for transfers between devices: 906 us -> none  [the longest x1 309 us: per_device(): lax.all_gather(left_power.astype(jnp.bfloat16), 'dp', axis=0, tiled=True)]
    reduce_scatter x1 -> x0, waiting for transfers between devices: 288 us -> none  [per_device(): lax.psum_scatter(summed / tokens_all, 'dp', scatter_dimension=0, tiled=True)]
    psum x2 -> x0, blocking collectives: 272 us -> none  [the longest x1 140 us: per_device(): total = lax.psum(jnp.sum(product * product), ('dp', 'tensor'))]
    all_to_all x0 -> x4, blocking collectives: none -> 99.9 us  [the longest x1 32 us: per_device(): totals = lax.all_to_all(total, DP + TENSOR, 0, 0, tiled=True)]
    dot_general x29 -> x2, matrix products: 44.9 us -> 0.94 us  [against(): lax.dot_general(left, right, (((0,), (0,)), ((), ())), preferred_element_...]
    all_to_all x0 -> x1, waiting for transfers between devices: none -> 23.7 us  [per_device(): lax.all_to_all(jnp.broadcast_to(tile[None], (plane, 512, 256)), PLANE, 0,...]
  transfers between devices with their start and end apart: 4 -> 2, of which waited for: 4 -> 2; matrix products, arithmetic and copies ran while one was open for 1% -> 0% of each run, Pallas kernels for 0% -> 0%
where the time goes in v1:
time: 156 us; the launch traced here: 155 us
  blocking collectives  99.9 us (64%)
  waiting for transfers between devices  25.7 us (16%)
  Pallas kernels  11 us (7%)
  starting transfers between devices  10.1 us (6%)
  local copies, waits for them, and re-layouts  4.63 us (3%)
    all_to_all x1, blocking collectives, per_device(): totals = lax.all_to_all(total, DP + TENSOR, 0, 0, tiled=True)  32 us
    all_to_all x1, blocking collectives, per_device(): lax.all_to_all(sent, PLANE, 0, 0, tiled=True).reshape(plane * tokens, 512)  29.1 us
    all_to_all x1, blocking collectives, per_device(): parts = lax.all_to_all(tile, 'z', 0, 0, tiled=True)  26.6 us
    all_to_all x1, waiting for transfers between devices, per_device(): lax.all_to_all(jnp.broadcast_to(tile[None], (plane, 512, 256)), PLANE, 0,...  23.7 us
    all_to_all x1, blocking collectives, per_device(): lax.all_to_all(jnp.broadcast_to(piece[None], (depth, 64, 256)), 'z', 0, 0...  12.1 us
    pallas_call x1, Pallas kernels, roots(): pl.pallas_call(roots_kernel, out_shape=(shape, shape, shape, jax.ShapeDty...  10.8 us
    ppermute x1, starting transfers between devices, per_device(): other = lax.ppermute(mine, 'core', [(0, 1), (1, 0)])  6.53 us
    all_to_all x1, starting transfers between devices, per_device(): lax.all_to_all(jnp.broadcast_to(tile[None], (plane, 512, 256)), PLANE, 0,...  3.6 us
  transfers between devices with their start and end apart: 2, of which 2 were waited for; matrix products, arithmetic and copies ran while one was open for 0% of the time, Pallas kernels for 0%

profile of v1, /device:TPU:1, one launch (start us, length us, event | category | flops | bytes accessed | tf_op | source)
XLA Modules:
  0.0 155.1 jit_solution(17428121549801311239)
XLA Ops:
  0.6 0.0 copy-start
  0.6 1.0 copy-done
  1.7 0.0 copy-start.1
  1.7 1.0 copy-done.1
  2.7 0.2 shard_map.49
  2.9 29.1 %all_to_all.32 = bf16[8,256,512]{2,1,0:T(8,128)(2,1)S(1)} all-to-all(bf16[8,256,512]{2,1,0:T(8,128)(2,1)S(1)} %shard_map.49), channel_id=1, replica_groups=mesh['x'=4,'z'=8,'yl'=2,'yh'=4,'core'=2] {'x','yl'}, dimensions={0} | all-to-all | bytes 4194304 | tf_op jit(solution)/shard_map/all_to_all | solution.py:145
  32.0 1.1 slice.12
  33.1 6.5 %collective-permute-start = (bf16[2048,256]{1,0:T(8,128)(2,1)}, bf16[2048,256]{1,0:T(8,128)(2,1)S(1)}, u32[]{:S(2)}, u32[]{:S(2)}) collective-permute-start(bf16[2048,256]{1,0:T(8,128)(2,1)} %slice.12), channel_id=1, source_target_pairs={{0,1},{1,0},{2,3},{3,2},{4,5},{5,4},{6,7},{7,6},{8,9},{9,8},{10,11... | collective-permute-start | bytes 3145736 | tf_op jit(solution)/shard_map/ppermute | solution.py:147
  39.6 0.5 fusion.2
  40.1 2.0 %collective-permute-done = bf16[2048,256]{1,0:T(8,128)(2,1)S(1)} collective-permute-done((bf16[2048,256]{1,0:T(8,128)(2,1)}, bf16[2048,256]{1,0:T(8,128)(2,1)S(1)}, u32[]{:S(2)}, u32[]{:S(2)}) %collective-permute-start) | collective-permute-done | bytes 1048608 | tf_op jit(solution)/shard_map/ppermute | solution.py:147
  42.1 0.5 fusion
  42.6 26.6 %all_to_all.33 = f32[8,64,256]{2,1,0:T(8,128)S(1)} all-to-all(f32[8,64,256]{2,1,0:T(8,128)S(1)} %bitcast.14), channel_id=1, replica_groups=mesh['x'=4,'z'=8,'yl'=2,'yh'=4,'core'=2] {'z'}, dimensions={0} | all-to-all | bytes 1048576 | tf_op jit(solution)/shard_map/all_to_all | solution.py:152
  69.3 12.1 %all_to_all.34 = bf16[8,64,256]{2,1,0:T(8,128)(2,1)S(1)} all-to-all(bf16[8,64,256]{2,1,0:T(8,128)(2,1)S(1)} %broadcast_in_dim.6), channel_id=1, replica_groups=mesh['x'=4,'z'=8,'yl'=2,'yh'=4,'core'=2] {'z'}, dimensions={0} | all-to-all | bytes 524288 | tf_op jit(solution)/shard_map/all_to_all | solution.py:154
  81.4 1.5 broadcast_in_dim.15
  82.9 3.6 %all-to-all-start.3 = ((bf16[8,512,256]{2,1,0:T(8,128)(2,1)}), bf16[8,512,256]{2,1,0:T(8,128)(2,1)S(1)}, u32[]{:S(2)}, u32[]{:S(2)}) async-start(bf16[8,512,256]{2,1,0:T(8,128)(2,1)} %broadcast_in_dim.15), calls=%async_computation.3 | async-start | bytes 4194304 | tf_op jit(solution)/shard_map/all_to_all | solution.py:156
  86.5 23.7 %all-to-all-done.3.tiles_ref = bf16[8,512,256]{2,1,0:T(8,128)(2,1)S(1)} async-done(((bf16[8,512,256]{2,1,0:T(8,128)(2,1)}), bf16[8,512,256]{2,1,0:T(8,128)(2,1)S(1)}, u32[]{:S(2)}, u32[]{:S(2)}) %all-to-all-start.3) | async-done | bytes 2097184 | tf_op jit(solution)/shard_map/all_to_all | solution.py:156
  110.2 10.8 %shard_map.50 = (f32[16,1024]{1,0:T(8,128)}, f32[16,1024]{1,0:T(8,128)}, f32[16,1024]{1,0:T(8,128)S(1)}, f32[512,128]{1,0:T(8,128)S(1)}) custom-call(s32[1]{0:T(128)} %bitcast.start_ref, bf16[8,512,256]{2,1,0:T(8,128)(2,1)S(1)} %all-to-all-done.3.tiles_ref), custom_call_target="tpu_custom_call" | custom-call | tf_op jit(solution)/shard_map/pallas_call | solution.py:103
  121.1 32.0 %all_to_all.35 = f32[512,1,128]{2,1,0:T(1,128)S(1)} all-to-all(f32[512,1,128]{2,1,0:T(1,128)S(1)} %bitcast.10), channel_id=1, replica_groups=mesh['x'=4,'z'=8,'yl'=2,'yh'=4,'core'=2] {'x','z','yl','yh','core'}, dimensions={0} | all-to-all | bytes 524288 | tf_op jit(solution)/shard_map/all_to_all | solution.py:161
  153.1 0.7 slice_reduce_fusion
  154.5 0.6 broadcast_multiply_fusion
  (4 shorter events, 0.1 us)
Async XLA Ops:
  0.6 1.0 copy-start
  1.7 1.0 copy-start.1
  33.1 9.0 %collective-permute-start = (bf16[2048,256]{1,0:T(8,128)(2,1)}, bf16[2048,256]{1,0:T(8,128)(2,1)S(1)}, u32[]{:S(2)}, u32[]{:S(2)}) collective-permute-start(bf16[2048,256]{1,0:T(8,128)(2,1)} %slice.12), channel_id=1, source_target_pairs={{0,1},{1,0},{2,3},{3,2},{4,5},{5,4},{6,7},{7,6},{8,9},{9,8},{10,11... | collective-permute-start | bytes 3145736 | tf_op jit(solution)/shard_map/ppermute | solution.py:147
  82.9 27.4 %all-to-all-start.3 = ((bf16[8,512,256]{2,1,0:T(8,128)(2,1)}), bf16[8,512,256]{2,1,0:T(8,128)(2,1)S(1)}, u32[]{:S(2)}, u32[]{:S(2)}) async-start(bf16[8,512,256]{2,1,0:T(8,128)(2,1)} %broadcast_in_dim.15), calls=%async_computation.3 | async-start | bytes 4194304 | tf_op jit(solution)/shard_map/all_to_all | solution.py:156

commit v2 on v1

--- a/solution.py
+++ b/solution.py
@@ -6,30 +6,38 @@
 from jax.sharding import Mesh, PartitionSpec as P
 
 DAMPING = 1e-06
-SIZES = (4, 8, 2, 4, 2)
-NAMES = ("x", "z", "yl", "yh", "core")
-DP = ("x", "z", "yl")
+SIZES = (4, 4, 2, 2, 4, 2)
+NAMES = ("x", "zh", "zl", "yl", "yh", "core")
+DP = ("x", "zh", "zl", "yl")
 TENSOR = ("yh", "core")
 PLANE = ("x", "yl")
+DEPTH = ("zh", "zl")
+SPREAD = ("x", "zl", "yl", "yh", "core")
 F32 = jnp.float32
 LOW = jnp.bfloat16
 
 
+def parts_of(vector):
+    high = vector.astype(LOW)
+    rest = (vector - high.astype(F32)).astype(LOW)
+    return jnp.concatenate([high, rest], axis=0)
+
+
 def times(vector, weight):
     rows = vector.shape[0]
-    high = vector.astype(LOW)
-    rest = (vector - high.astype(F32)).astype(LOW)
-    both = jnp.dot(
-        jnp.concatenate([high, rest], axis=0), weight, preferred_element_type=F32
-    )
+    both = jnp.dot(parts_of(vector), weight, preferred_element_type=F32)
     return both[:rows] + both[rows:]
 
 
-def roots_kernel(start_ref, tiles_ref, left_ref, right_ref, product_ref, total_ref, grad, flip):
+def roots_kernel(tiles_ref, left_ref, right_ref, product_ref, total_ref, grad, flip, keep):
     width = grad.shape[0]
     rows = left_ref.shape[0]
     n_tiles, high, wide = tiles_ref.shape
-    start = pl.multiple_of(start_ref[0], rows)
+    groups = keep.shape[0] // rows
+    first = (lax.axis_index("x") * 16 + lax.axis_index("zl") * 2 + lax.axis_index("yl")) * rows
+    starts = [pl.multiple_of(first + group * (4 * rows), rows) for group in range(groups)]
+    mine = pl.multiple_of(lax.axis_index("zh") * rows, rows)
+    start = pl.multiple_of(first + lax.axis_index("zh") * (4 * rows), rows)
     for index in range(n_tiles):
         col, row = index // 2, index % 2
         grad[row * high : (row + 1) * high, col * wide : (col + 1) * wide] = tiles_ref[index]
@@ -52,7 +60,9 @@
 
     col_index = lax.broadcasted_iota(jnp.int32, (rows, width), 1)
     row_index = lax.broadcasted_iota(jnp.int32, (rows, width), 0)
-    eye = (col_index == start + row_index).astype(F32)
+
+    def eye_of(begin):
+        return (col_index == begin + row_index).astype(F32)
 
     def finish(vector, outer):
         return (outer + DAMPING * vector) * inverse
@@ -63,23 +73,26 @@
     def left_power(vector):
         return finish(vector, times(times(vector, grad[...]), flip[...]))
 
-    first = jnp.dot(grad[pl.ds(start, rows), :], flip[...], preferred_element_type=F32)
-    root = stepped(eye, finish(eye, first))
+    eyes = jnp.concatenate([eye_of(begin) for begin in starts], axis=0)
+    chosen = jnp.concatenate([grad[pl.ds(begin, rows), :] for begin in starts], axis=0)
+    outer = jnp.dot(chosen, flip[...], preferred_element_type=F32)
+    root = stepped(eyes, finish(eyes, outer))
     vector = root
     for _ in range(4):
         vector = stepped(vector, left_power(vector))
     left = stepped(root, left_power(vector))
-    left_ref[...] = left
+    keep[...] = left
+    left_ref[...] = keep[pl.ds(mine, rows), :]
 
-    high_left = left.astype(LOW)
-    rest_left = (left - high_left.astype(F32)).astype(LOW)
+    eye = eye_of(start)
+    count = groups * rows
     both = jnp.dot(
-        jnp.concatenate([high_left, rest_left, flip[pl.ds(start, rows), :]], axis=0),
+        jnp.concatenate([parts_of(left), flip[pl.ds(start, rows), :]], axis=0),
         grad[...],
         preferred_element_type=F32,
     )
-    product = both[:rows] + both[rows : 2 * rows]
-    right = stepped(eye, finish(eye, both[2 * rows :]))
+    product = both[:count] + both[count : 2 * count]
+    right = stepped(eye, finish(eye, both[2 * count :]))
 
     def right_power(vector):
         return finish(vector, times(times(vector, flip[...]), grad[...]))
@@ -92,22 +105,27 @@
     root = stepped(root, right_power(vector))
     right_ref[...] = root[:rows]
     product = root[rows:]
-    product_ref[...] = product
     total_ref[...] = jnp.full(total_ref.shape, jnp.sum(product * product), F32)
+    keep[...] = product
+    product_ref[...] = keep[pl.ds(mine, rows), :]
 
 
-def roots(start, tiles, rows, devices):
+def roots(tiles, rows, devices):
     width = 1024
     shape = jax.ShapeDtypeStruct((rows, width), F32)
     vmem = pl.BlockSpec(memory_space=pltpu.VMEM)
     return pl.pallas_call(
         roots_kernel,
         out_shape=(shape, shape, shape, jax.ShapeDtypeStruct((devices, 128), F32)),
-        in_specs=[pl.BlockSpec(memory_space=pltpu.SMEM), vmem],
+        in_specs=[vmem],
         out_specs=(vmem, vmem, vmem, vmem),
-        scratch_shapes=[pltpu.VMEM((width, width), LOW), pltpu.VMEM((width, width), LOW)],
+        scratch_shapes=[
+            pltpu.VMEM((width, width), LOW),
+            pltpu.VMEM((width, width), LOW),
+            pltpu.VMEM((4 * rows, width), F32),
+        ],
         compiler_params=pltpu.CompilerParams(vmem_limit_bytes=32 * 1024 * 1024),
-    )(start, tiles)
+    )(tiles)
 
 
 def pack_kernel(core_ref, acts_ref, grad_ref, sent_ref):
@@ -149,16 +167,15 @@
     tile = jnp.where(
         core == 0, jnp.concatenate([mine, other]), jnp.concatenate([other, mine])
     ).reshape(depth, 64, 256)
-    parts = lax.all_to_all(tile, "z", 0, 0, tiled=True)
+    parts = lax.all_to_all(tile, DEPTH, 0, 0, tiled=True)
     piece = (jnp.sum(parts, axis=0) / (tokens * owners)).astype(LOW)
-    tile = lax.all_to_all(jnp.broadcast_to(piece[None], (depth, 64, 256)), "z", 0, 0, tiled=True)
+    tile = lax.all_to_all(jnp.broadcast_to(piece[None], (depth, 64, 256)), DEPTH, 0, 0, tiled=True)
     tile = tile.reshape(512, 256)
     tiles = lax.all_to_all(
         jnp.broadcast_to(tile[None], (plane, 512, 256)), PLANE, 0, 0, tiled=True
     )
-    start = (lax.axis_index(DP) * rows).astype(jnp.int32).reshape(1)
-    left, right, product, total = roots(start, tiles, rows, 512)
-    totals = lax.all_to_all(total, DP + TENSOR, 0, 0, tiled=True)
+    left, right, product, total = roots(tiles, rows, 128)
+    totals = lax.all_to_all(total, SPREAD, 0, 0, tiled=True)
     mean = jnp.sum(totals[:, 0]) / (width * width * 8)
     update = product * lax.rsqrt(mean + 1e-06)
     return (left, right, update)

time: 156 us -> 143 us (0.917)
  waiting for transfers between devices: 25.7 us -> 2 us
  blocking collectives: 99.9 us -> 116 us
  starting transfers between devices: 10.1 us -> 6.53 us
    all_to_all x1 -> x0, waiting for transfers between devices: 23.7 us -> none  [per_device(): lax.all_to_all(jnp.broadcast_to(tile[None], (plane, 512, 256)), PLANE, 0,...]
    all_to_all x3 -> x4, blocking collectives: 70.7 us -> 87.3 us  [the longest x1 26.6 us: per_device(): parts = lax.all_to_all(tile, DEPTH, 0, 0, tiled=True)]
    all_to_all x1 -> x0, starting transfers between devices: 3.6 us -> none  [per_device(): lax.all_to_all(jnp.broadcast_to(tile[None], (plane, 512, 256)), PLANE, 0,...]
  transfers between devices with their start and end apart: 2 -> 1, of which waited for: 2 -> 1; matrix products, arithmetic and copies ran while one was open for 0% -> 0% of each run, Pallas kernels for 0% -> 0%
where the time goes in v2:
time: 143 us
  blocking collectives  116 us (81%)
  Pallas kernels  11.1 us (8%)
  starting transfers between devices  6.53 us (5%)
  local copies, waits for them, and re-layouts  3.29 us (2%)
  waiting for transfers between devices  2 us (1%)
    all_to_all x1, blocking collectives, per_device(): lax.all_to_all(sent, PLANE, 0, 0, tiled=True).reshape(plane * tokens, 512)  29.1 us
    all_to_all x1, blocking collectives, per_device(): parts = lax.all_to_all(tile, DEPTH, 0, 0, tiled=True)  26.6 us
    all_to_all x1, blocking collectives, per_device(): lax.all_to_all(jnp.broadcast_to(tile[None], (plane, 512, 256)), PLANE, 0,...  26.1 us
    all_to_all x1, blocking collectives, per_device(): totals = lax.all_to_all(total, SPREAD, 0, 0, tiled=True)  22.7 us
    all_to_all x1, blocking collectives, per_device(): lax.all_to_all(jnp.broadcast_to(piece[None], (depth, 64, 256)), DEPTH, 0,...  11.9 us
    pallas_call x1, Pallas kernels, roots(): pl.pallas_call(roots_kernel, out_shape=(shape, shape, shape, jax.ShapeDty...  10.9 us
    ppermute x1, starting transfers between devices, per_device(): other = lax.ppermute(mine, 'core', [(0, 1), (1, 0)])  6.53 us
  transfers between devices with their start and end apart: 1, of which 1 were waited for; matrix products, arithmetic and copies ran while one was open for 0% of the time, Pallas kernels for 0%

profile of v2, /device:TPU:1, one launch (start us, length us, event | category | flops | bytes accessed | tf_op | source)
XLA Modules:
  0.0 143.1 jit_solution(17298895304046214706)
XLA Ops:
  0.6 0.0 copy-start
  0.6 1.0 copy-done
  1.7 0.0 copy-start.1
  1.7 1.0 copy-done.1
  2.7 0.2 shard_map.49
  2.9 29.1 %all_to_all.32 = bf16[8,256,512]{2,1,0:T(8,128)(2,1)S(1)} all-to-all(bf16[8,256,512]{2,1,0:T(8,128)(2,1)S(1)} %shard_map.49), channel_id=1, replica_groups=mesh['x'=4,'zh'=4,'zl'=2,'yl'=2,'yh'=4,'core'=2] {'x','yl'}, dimensions={0} | all-to-all | bytes 4194304 | tf_op jit(solution)/shard_map/all_to_all | solution.py:163
  32.0 1.1 slice.12
  33.1 6.5 %collective-permute-start = (bf16[2048,256]{1,0:T(8,128)(2,1)}, bf16[2048,256]{1,0:T(8,128)(2,1)S(1)}, u32[]{:S(2)}, u32[]{:S(2)}) collective-permute-start(bf16[2048,256]{1,0:T(8,128)(2,1)} %slice.12), channel_id=1, source_target_pairs={{0,1},{1,0},{2,3},{3,2},{4,5},{5,4},{6,7},{7,6},{8,9},{9,8},{10,11... | collective-permute-start | bytes 3145736 | tf_op jit(solution)/shard_map/ppermute | solution.py:165
  39.6 0.5 fusion.2
  40.1 2.0 %collective-permute-done = bf16[2048,256]{1,0:T(8,128)(2,1)S(1)} collective-permute-done((bf16[2048,256]{1,0:T(8,128)(2,1)}, bf16[2048,256]{1,0:T(8,128)(2,1)S(1)}, u32[]{:S(2)}, u32[]{:S(2)}) %collective-permute-start) | collective-permute-done | bytes 1048608 | tf_op jit(solution)/shard_map/ppermute | solution.py:165
  42.1 0.5 fusion
  42.6 26.6 %all_to_all.33 = f32[8,64,256]{2,1,0:T(8,128)S(1)} all-to-all(f32[8,64,256]{2,1,0:T(8,128)S(1)} %bitcast.13), channel_id=1, replica_groups=mesh['x'=4,'zh'=4,'zl'=2,'yl'=2,'yh'=4,'core'=2] {'zh','zl'}, dimensions={0} | all-to-all | bytes 1048576 | tf_op jit(solution)/shard_map/all_to_all | solution.py:170
  69.3 11.9 %all_to_all.34 = bf16[8,64,256]{2,1,0:T(8,128)(2,1)S(1)} all-to-all(bf16[8,64,256]{2,1,0:T(8,128)(2,1)S(1)} %broadcast_in_dim.6), channel_id=1, replica_groups=mesh['x'=4,'zh'=4,'zl'=2,'yl'=2,'yh'=4,'core'=2] {'zh','zl'}, dimensions={0} | all-to-all | bytes 524288 | tf_op jit(solution)/shard_map/all_to_all | solution.py:172
  81.2 0.1 broadcast_in_dim.15
  81.3 26.1 %all_to_all.35.tiles_ref = bf16[8,512,256]{2,1,0:T(8,128)(2,1)S(1)} all-to-all(bf16[8,512,256]{2,1,0:T(8,128)(2,1)S(1)} %broadcast_in_dim.15), channel_id=1, replica_groups=mesh['x'=4,'zh'=4,'zl'=2,'yl'=2,'yh'=4,'core'=2] {'x','yl'}, dimensions={0} | all-to-all | bytes 4194304 | tf_op jit(solution)/shard_map/all_to_all | solution.py:174
  107.4 10.9 %shard_map.50 = (f32[16,1024]{1,0:T(8,128)}, f32[16,1024]{1,0:T(8,128)}, f32[16,1024]{1,0:T(8,128)S(1)}, f32[128,128]{1,0:T(8,128)S(1)}) custom-call(bf16[8,512,256]{2,1,0:T(8,128)(2,1)S(1)} %all_to_all.35.tiles_ref), custom_call_target="tpu_custom_call" | custom-call | tf_op jit(solution)/shard_map/pallas_call | solution.py:117
  118.4 22.7 %all_to_all.36 = f32[128,1,128]{2,1,0:T(1,128)S(1)} all-to-all(f32[128,1,128]{2,1,0:T(1,128)S(1)} %bitcast.9), channel_id=1, replica_groups=mesh['x'=4,'zh'=4,'zl'=2,'yl'=2,'yh'=4,'core'=2] {'x','zl','yl','yh','co..., dimensions={0} | all-to-all | bytes 131072 | tf_op jit(solution)/shard_map/all_to_all | solution.py:178
  141.1 0.6 slice_reduce_fusion
  142.4 0.6 broadcast_multiply_fusion
  (4 shorter events, 0.1 us)
Async XLA Ops:
  0.6 1.0 copy-start
  1.7 1.0 copy-start.1
  33.1 9.0 %collective-permute-start = (bf16[2048,256]{1,0:T(8,128)(2,1)}, bf16[2048,256]{1,0:T(8,128)(2,1)S(1)}, u32[]{:S(2)}, u32[]{:S(2)}) collective-permute-start(bf16[2048,256]{1,0:T(8,128)(2,1)} %slice.12), channel_id=1, source_target_pairs={{0,1},{1,0},{2,3},{3,2},{4,5},{5,4},{6,7},{7,6},{8,9},{9,8},{10,11... | collective-permute-start | bytes 3145736 | tf_op jit(solution)/shard_map/ppermute | solution.py:165

commit v3 on v2

--- a/solution.py
+++ b/solution.py
@@ -15,6 +15,7 @@
 SPREAD = ("x", "zl", "yl", "yh", "core")
 F32 = jnp.float32
 LOW = jnp.bfloat16
+ACROSS = (((1,), (1,)), ((), ()))
 
 
 def parts_of(vector):
@@ -29,11 +30,14 @@
     return both[:rows] + both[rows:]
 
 
-def roots_kernel(tiles_ref, left_ref, right_ref, product_ref, total_ref, grad, flip, keep):
+def roots_kernel(
+    tiles_ref, left_ref, right_ref, product_ref, total_ref, grad, stat, rest, turned, keep
+):
     width = grad.shape[0]
     rows = left_ref.shape[0]
     n_tiles, high, wide = tiles_ref.shape
     groups = keep.shape[0] // rows
+    count = groups * rows
     first = (lax.axis_index("x") * 16 + lax.axis_index("zl") * 2 + lax.axis_index("yl")) * rows
     starts = [pl.multiple_of(first + group * (4 * rows), rows) for group in range(groups)]
     mine = pl.multiple_of(lax.axis_index("zh") * rows, rows)
@@ -41,22 +45,51 @@
     for index in range(n_tiles):
         col, row = index // 2, index % 2
         grad[row * high : (row + 1) * high, col * wide : (col + 1) * wide] = tiles_ref[index]
-    for row in range(0, width, 256):
-        for col in range(0, width, 256):
-            flip[col : col + 256, row : row + 256] = grad[
-                row : row + 256, col : col + 256
-            ].T
-    total = jnp.zeros((256, 256), F32)
-    trace = jnp.zeros((256, width), F32)
-    for row in range(0, width, 256):
-        part = grad[row : row + 256, :]
-        wide_part = part.astype(F32)
-        trace += wide_part * wide_part
-        for col in range(row, width, 256):
-            stat = jnp.dot(part, flip[:, col : col + 256], preferred_element_type=F32)
-            total += (1.0 if col == row else 2.0) * (stat * stat)
-    square = jnp.sum(total) + 2.0 * DAMPING * jnp.sum(trace) + width * DAMPING * DAMPING
-    inverse = lax.rsqrt(jnp.full((1, 1), square, F32))
+
+    side = 256
+    on_diagonal = lax.broadcasted_iota(jnp.int32, (side, side), 0) == lax.broadcasted_iota(
+        jnp.int32, (side, side), 1
+    )
+    squares = crossed = squared = jnp.zeros((side, side), F32)
+    diagonal, rounded = [], []
+    for row in range(0, width, side):
+        part = grad[row : row + side, :]
+        for col in range(row, width, side):
+            tile = lax.dot_general(
+                part, grad[col : col + side, :], ACROSS, preferred_element_type=F32
+            )
+            tile_low = tile.astype(LOW)
+            back = tile_low.astype(F32)
+            tile_rest = (tile - back).astype(LOW)
+            stat[row : row + side, col : col + side] = tile_low
+            rest[row : row + side, col : col + side] = tile_rest
+            if col > row:
+                stat[col : col + side, row : row + side] = tile_low.T
+                rest[col : col + side, row : row + side] = tile_rest.T
+                squares += 2.0 * (tile * tile)
+                crossed += tile * back
+                squared += back * back
+            else:
+                outside = jnp.where(on_diagonal, 0.0, back)
+                damped = jnp.where(on_diagonal, tile + DAMPING, tile)
+                squares += damped * damped
+                crossed += 0.5 * (tile * outside)
+                squared += 0.5 * (outside * outside)
+                diagonal.append(jnp.sum(jnp.where(on_diagonal, tile, 0.0), axis=0, keepdims=True))
+                rounded.append(jnp.sum(jnp.where(on_diagonal, back, 0.0), axis=0, keepdims=True))
+    inverse = lax.rsqrt(jnp.full((1, 1), jnp.sum(squares), F32))
+    above = jnp.full((1, 1), jnp.sum(crossed), F32)
+    below = jnp.full((1, 1), jnp.sum(squared), F32)
+    gain = jnp.where(below > 0.0, above / jnp.where(below > 0.0, below, 1.0), 1.0)
+    delta = DAMPING * inverse
+    tau = 1.25 - 0.25 * delta
+    own = tau - (0.25 * inverse) * (
+        jnp.concatenate(diagonal, axis=1) - gain * jnp.concatenate(rounded, axis=1)
+    )
+    shared = 0.25 * inverse * gain
+
+    def stepped(vector):
+        return own * vector - shared * times(vector, stat[...])
 
     col_index = lax.broadcasted_iota(jnp.int32, (rows, width), 1)
     row_index = lax.broadcasted_iota(jnp.int32, (rows, width), 0)
@@ -64,47 +97,41 @@
     def eye_of(begin):
         return (col_index == begin + row_index).astype(F32)
 
-    def finish(vector, outer):
-        return (outer + DAMPING * vector) * inverse
-
-    def stepped(vector, power):
-        return (5.0 * vector - power) * 0.25
-
-    def left_power(vector):
-        return finish(vector, times(times(vector, grad[...]), flip[...]))
+    def chosen(begin):
+        return stat[pl.ds(begin, rows), :].astype(F32) + rest[pl.ds(begin, rows), :].astype(F32)
 
     eyes = jnp.concatenate([eye_of(begin) for begin in starts], axis=0)
-    chosen = jnp.concatenate([grad[pl.ds(begin, rows), :] for begin in starts], axis=0)
-    outer = jnp.dot(chosen, flip[...], preferred_element_type=F32)
-    root = stepped(eyes, finish(eyes, outer))
-    vector = root
-    for _ in range(4):
-        vector = stepped(vector, left_power(vector))
-    left = stepped(root, left_power(vector))
+    power = jnp.concatenate([chosen(begin) for begin in starts], axis=0)
+    power = (power + DAMPING * eyes) * inverse
+    block = pl.multiple_of(start // 128 * 128, 128)
+    turned[...] = grad[:, pl.ds(block, 128)].T
+    column = turned[pl.ds(pl.multiple_of(start - block, rows), rows), :].astype(F32)
+    small = 0.0625 * delta
+    square = tau * tau
+    factors = [small * (square * tau), small * square, small * tau, small]
+    vector = jnp.concatenate([power, column], axis=0)
+    inner = (0.3125 - small * (square * square)) * column
+    for factor in factors:
+        vector = stepped(vector)
+        inner -= factor * vector[count:]
+    vector = stepped(vector)
+    inner += 0.25 * vector[count:]
+    left = 1.5625 * eyes - (0.3125 * power + 0.25 * vector[:count])
     keep[...] = left
     left_ref[...] = keep[pl.ds(mine, rows), :]
 
-    eye = eye_of(start)
-    count = groups * rows
-    both = jnp.dot(
-        jnp.concatenate([parts_of(left), flip[pl.ds(start, rows), :]], axis=0),
-        grad[...],
-        preferred_element_type=F32,
-    )
-    product = both[:count] + both[count : 2 * count]
-    right = stepped(eye, finish(eye, both[2 * count :]))
-
-    def right_power(vector):
-        return finish(vector, times(times(vector, flip[...]), grad[...]))
-
-    product = stepped(product, right_power(product))
-    root = jnp.concatenate([right, product], axis=0)
-    vector = root
-    for _ in range(4):
-        vector = stepped(vector, right_power(vector))
-    root = stepped(root, right_power(vector))
-    right_ref[...] = root[:rows]
-    product = root[rows:]
+    power = times(left, stat[...]) + jnp.dot(
+        left.astype(LOW), rest[...], preferred_element_type=F32
+    )
+    power = (power + DAMPING * left) * inverse
+    vector = power
+    for _ in range(5):
+        vector = stepped(vector)
+    twice = 1.5625 * left - (0.3125 * power + 0.25 * vector)
+    out = times(jnp.concatenate([inner, twice], axis=0), grad[...])
+    base = 1.5625 - delta * (0.3125 + 0.25 * (square * square * tau))
+    right_ref[...] = base * eye_of(start) - inverse * out[:rows]
+    product = out[rows:]
     total_ref[...] = jnp.full(total_ref.shape, jnp.sum(product * product), F32)
     keep[...] = product
     product_ref[...] = keep[pl.ds(mine, rows), :]
@@ -122,6 +149,8 @@
         scratch_shapes=[
             pltpu.VMEM((width, width), LOW),
             pltpu.VMEM((width, width), LOW),
+            pltpu.VMEM((width, width), LOW),
+            pltpu.VMEM((128, width), LOW),
             pltpu.VMEM((4 * rows, width), F32),
         ],
         compiler_params=pltpu.CompilerParams(vmem_limit_bytes=32 * 1024 * 1024),

time: 143 us -> 141 us (0.986)
  Pallas kernels: 11.1 us -> 8.21 us
    pallas_call x1, Pallas kernels: 10.9 us -> 8.06 us  [roots(): pl.pallas_call(roots_kernel, out_shape=(shape, shape, shape, jax.ShapeDty...]
where the time goes in v3:
time: 141 us; the launch traced here: 140 us
  blocking collectives  116 us (82%)
  Pallas kernels  8.21 us (6%)
  starting transfers between devices  6.53 us (5%)
  local copies, waits for them, and re-layouts  3.29 us (2%)
  waiting for transfers between devices  2 us (1%)
  between operations  1.41 us (1%)
    all_to_all x1, blocking collectives, per_device(): lax.all_to_all(sent, PLANE, 0, 0, tiled=True).reshape(plane * tokens, 512)  29.1 us
    all_to_all x1, blocking collectives, per_device(): parts = lax.all_to_all(tile, DEPTH, 0, 0, tiled=True)  26.6 us
    all_to_all x1, blocking collectives, per_device(): lax.all_to_all(jnp.broadcast_to(tile[None], (plane, 512, 256)), PLANE, 0,...  26.1 us
    all_to_all x1, blocking collectives, per_device(): totals = lax.all_to_all(total, SPREAD, 0, 0, tiled=True)  22.7 us
    all_to_all x1, blocking collectives, per_device(): lax.all_to_all(jnp.broadcast_to(piece[None], (depth, 64, 256)), DEPTH, 0,...  11.9 us
    pallas_call x1, Pallas kernels, roots(): pl.pallas_call(roots_kernel, out_shape=(shape, shape, shape, jax.ShapeDty...  8.06 us
    ppermute x1, starting transfers between devices, per_device(): other = lax.ppermute(mine, 'core', [(0, 1), (1, 0)])  6.53 us
  transfers between devices with their start and end apart: 1, of which 1 were waited for; matrix products, arithmetic and copies ran while one was open for 0% of the time, Pallas kernels for 0%

profile of v3, /device:TPU:1, one launch (start us, length us, event | category | flops | bytes accessed | tf_op | source)
XLA Modules:
  0.0 140.2 jit_solution(15586213395323873005)
XLA Ops:
  0.6 0.0 copy-start
  0.6 1.0 copy-done
  1.7 0.0 copy-start.1
  1.7 1.0 copy-done.1
  2.7 0.2 shard_map.49
  2.9 29.1 %all_to_all.32 = bf16[8,256,512]{2,1,0:T(8,128)(2,1)S(1)} all-to-all(bf16[8,256,512]{2,1,0:T(8,128)(2,1)S(1)} %shard_map.49), channel_id=1, replica_groups=mesh['x'=4,'zh'=4,'zl'=2,'yl'=2,'yh'=4,'core'=2] {'x','yl'}, dimensions={0} | all-to-all | bytes 4194304 | tf_op jit(solution)/shard_map/all_to_all | solution.py:192
  32.0 1.1 slice.12
  33.1 6.5 %collective-permute-start = (bf16[2048,256]{1,0:T(8,128)(2,1)}, bf16[2048,256]{1,0:T(8,128)(2,1)S(1)}, u32[]{:S(2)}, u32[]{:S(2)}) collective-permute-start(bf16[2048,256]{1,0:T(8,128)(2,1)} %slice.12), channel_id=1, source_target_pairs={{0,1},{1,0},{2,3},{3,2},{4,5},{5,4},{6,7},{7,6},{8,9},{9,8},{10,11... | collective-permute-start | bytes 3145736 | tf_op jit(solution)/shard_map/ppermute | solution.py:194
  39.6 0.5 fusion.2
  40.1 2.0 %collective-permute-done = bf16[2048,256]{1,0:T(8,128)(2,1)S(1)} collective-permute-done((bf16[2048,256]{1,0:T(8,128)(2,1)}, bf16[2048,256]{1,0:T(8,128)(2,1)S(1)}, u32[]{:S(2)}, u32[]{:S(2)}) %collective-permute-start) | collective-permute-done | bytes 1048608 | tf_op jit(solution)/shard_map/ppermute | solution.py:194
  42.1 0.5 fusion
  42.6 26.6 %all_to_all.33 = f32[8,64,256]{2,1,0:T(8,128)S(1)} all-to-all(f32[8,64,256]{2,1,0:T(8,128)S(1)} %bitcast.13), channel_id=1, replica_groups=mesh['x'=4,'zh'=4,'zl'=2,'yl'=2,'yh'=4,'core'=2] {'zh','zl'}, dimensions={0} | all-to-all | bytes 1048576 | tf_op jit(solution)/shard_map/all_to_all | solution.py:199
  69.3 11.9 %all_to_all.34 = bf16[8,64,256]{2,1,0:T(8,128)(2,1)S(1)} all-to-all(bf16[8,64,256]{2,1,0:T(8,128)(2,1)S(1)} %broadcast_in_dim.6), channel_id=1, replica_groups=mesh['x'=4,'zh'=4,'zl'=2,'yl'=2,'yh'=4,'core'=2] {'zh','zl'}, dimensions={0} | all-to-all | bytes 524288 | tf_op jit(solution)/shard_map/all_to_all | solution.py:201
  81.2 0.1 broadcast_in_dim.15
  81.3 26.1 %all_to_all.35.tiles_ref = bf16[8,512,256]{2,1,0:T(8,128)(2,1)S(1)} all-to-all(bf16[8,512,256]{2,1,0:T(8,128)(2,1)S(1)} %broadcast_in_dim.15), channel_id=1, replica_groups=mesh['x'=4,'zh'=4,'zl'=2,'yl'=2,'yh'=4,'core'=2] {'x','yl'}, dimensions={0} | all-to-all | bytes 4194304 | tf_op jit(solution)/shard_map/all_to_all | solution.py:203
  107.4 8.1 %shard_map.50 = (f32[16,1024]{1,0:T(8,128)}, f32[16,1024]{1,0:T(8,128)}, f32[16,1024]{1,0:T(8,128)S(1)}, f32[128,128]{1,0:T(8,128)S(1)}) custom-call(bf16[8,512,256]{2,1,0:T(8,128)(2,1)S(1)} %all_to_all.35.tiles_ref), custom_call_target="tpu_custom_call" | custom-call | tf_op jit(solution)/shard_map/pallas_call | solution.py:144
  115.5 22.7 %all_to_all.36 = f32[128,1,128]{2,1,0:T(1,128)S(1)} all-to-all(f32[128,1,128]{2,1,0:T(1,128)S(1)} %bitcast.9), channel_id=1, replica_groups=mesh['x'=4,'zh'=4,'zl'=2,'yl'=2,'yh'=4,'core'=2] {'x','zl','yl','yh','co..., dimensions={0} | all-to-all | bytes 131072 | tf_op jit(solution)/shard_map/all_to_all | solution.py:207
  138.2 0.6 slice_reduce_fusion
  139.5 0.6 broadcast_multiply_fusion
  (4 shorter events, 0.1 us)
Async XLA Ops:
  0.6 1.0 copy-start
  1.7 1.0 copy-start.1
  33.1 9.0 %collective-permute-start = (bf16[2048,256]{1,0:T(8,128)(2,1)}, bf16[2048,256]{1,0:T(8,128)(2,1)S(1)}, u32[]{:S(2)}, u32[]{:S(2)}) collective-permute-start(bf16[2048,256]{1,0:T(8,128)(2,1)} %slice.12), channel_id=1, source_target_pairs={{0,1},{1,0},{2,3},{3,2},{4,5},{5,4},{6,7},{7,6},{8,9},{9,8},{10,11... | collective-permute-start | bytes 3145736 | tf_op jit(solution)/shard_map/ppermute | solution.py:194

commit v4 on v3

--- a/solution.py
+++ b/solution.py
@@ -157,26 +157,6 @@
     )(tiles)
 
 
-def pack_kernel(core_ref, acts_ref, grad_ref, sent_ref):
-    core = core_ref[0]
-    for index in range(sent_ref.shape[0]):
-        col, row = index // 2, index % 2
-        begin = pl.multiple_of(row * 512 + core * 256, 256)
-        sent_ref[index, :, :256] = acts_ref[:, pl.ds(begin, 256)]
-        sent_ref[index, :, 256:] = grad_ref[:, col * 256 : (col + 1) * 256]
-
-
-def pack(core, acts, up_grad, plane):
-    vmem = pl.BlockSpec(memory_space=pltpu.VMEM)
-    return pl.pallas_call(
-        pack_kernel,
-        out_shape=jax.ShapeDtypeStruct((plane, acts.shape[0], 512), LOW),
-        in_specs=[pl.BlockSpec(memory_space=pltpu.SMEM), vmem, vmem],
-        out_specs=vmem,
-        compiler_params=pltpu.CompilerParams(vmem_limit_bytes=16 * 1024 * 1024),
-    )(core.astype(jnp.int32).reshape(1), acts, up_grad)
-
-
 def against(left, right):
     return lax.dot_general(left, right, (((0,), (0,)), ((), ())), preferred_element_type=F32)
 
@@ -188,7 +168,15 @@
     plane = 8
     depth = 8
     core = lax.axis_index("core")
-    sent = pack(core, acts, up_grad, plane)
+    halves = [
+        lax.dynamic_slice_in_dim(acts, row * 512 + core * 256, 256, 1) for row in range(2)
+    ]
+    sent = jnp.stack(
+        [
+            jnp.concatenate([halves[i % 2], up_grad[:, i // 2 * 256 : i // 2 * 256 + 256]], axis=1)
+            for i in range(plane)
+        ]
+    )
     got = lax.all_to_all(sent, PLANE, 0, 0, tiled=True).reshape(plane * tokens, 512)
     mine, cols = got[:, :256], got[:, 256:]
     other = lax.ppermute(mine, "core", [(0, 1), (1, 0)])

time: 141 us -> 140 us (level)
    unnamed x4 -> x0, local copies, waits for them, and re-layouts: 2.08 us -> none
where the time goes in v4:
time: 140 us; the launch traced here: 139 us
  blocking collectives  116 us (83%)
  Pallas kernels  8.06 us (6%)
  starting transfers between devices  6.53 us (5%)
  local copies, waits for them, and re-layouts  2.49 us (2%)
  waiting for transfers between devices  2 us (1%)
  other arithmetic  1.49 us (1%)
  between operations  1.46 us (1%)
    all_to_all x1, blocking collectives, per_device(): lax.all_to_all(sent, PLANE, 0, 0, tiled=True).reshape(plane * tokens, 512)  29.1 us
    all_to_all x1, blocking collectives, per_device(): parts = lax.all_to_all(tile, DEPTH, 0, 0, tiled=True)  26.6 us
    all_to_all x1, blocking collectives, per_device(): lax.all_to_all(jnp.broadcast_to(tile[None], (plane, 512, 256)), PLANE, 0,...  26.3 us
    all_to_all x1, blocking collectives, per_device(): totals = lax.all_to_all(total, SPREAD, 0, 0, tiled=True)  22.3 us
    all_to_all x1, blocking collectives, per_device(): lax.all_to_all(jnp.broadcast_to(piece[None], (depth, 64, 256)), DEPTH, 0,...  12.1 us
    pallas_call x1, Pallas kernels, roots(): pl.pallas_call(roots_kernel, out_shape=(shape, shape, shape, jax.ShapeDty...  8.06 us
    ppermute x1, starting transfers between devices, per_device(): other = lax.ppermute(mine, 'core', [(0, 1), (1, 0)])  6.53 us
  transfers between devices with their start and end apart: 1, of which 1 were waited for; matrix products, arithmetic and copies ran while one was open for 0% of the time, Pallas kernels for 0%

profile of v4, /device:TPU:1, one launch (start us, length us, event | category | flops | bytes accessed | tf_op | source)
XLA Modules:
  0.0 139.4 jit_solution(14177023533396931721)
XLA Ops:
  0.6 1.3 constant_dynamic-slice_fusion
  2.1 29.1 %all_to_all.32 = bf16[8,256,512]{2,1,0:T(8,128)(2,1)S(1)} all-to-all(bf16[8,256,512]{2,1,0:T(8,128)(2,1)S(1)} %fusion.11), channel_id=1, replica_groups=mesh['x'=4,'zh'=4,'zl'=2,'yl'=2,'yh'=4,'core'=2] {'x','yl'}, dimensions={0} | all-to-all | bytes 4194304 | tf_op jit(solution)/shard_map/all_to_all | solution.py:180
  31.3 1.1 slice.32
  32.3 6.5 %collective-permute-start = (bf16[2048,256]{1,0:T(8,128)(2,1)}, bf16[2048,256]{1,0:T(8,128)(2,1)S(1)}, u32[]{:S(2)}, u32[]{:S(2)}) collective-permute-start(bf16[2048,256]{1,0:T(8,128)(2,1)} %slice.32), channel_id=1, source_target_pairs={{0,1},{1,0},{2,3},{3,2},{4,5},{5,4},{6,7},{7,6},{8,9},{9,8},{10,11... | collective-permute-start | bytes 3145736 | tf_op jit(solution)/shard_map/ppermute | solution.py:182
  38.9 0.5 fusion.2
  39.3 2.0 %collective-permute-done = bf16[2048,256]{1,0:T(8,128)(2,1)S(1)} collective-permute-done((bf16[2048,256]{1,0:T(8,128)(2,1)}, bf16[2048,256]{1,0:T(8,128)(2,1)S(1)}, u32[]{:S(2)}, u32[]{:S(2)}) %collective-permute-start) | collective-permute-done | bytes 1048608 | tf_op jit(solution)/shard_map/ppermute | solution.py:182
  41.3 0.5 fusion
  41.9 26.6 %all_to_all.33 = f32[8,64,256]{2,1,0:T(8,128)S(1)} all-to-all(f32[8,64,256]{2,1,0:T(8,128)S(1)} %bitcast.44), channel_id=1, replica_groups=mesh['x'=4,'zh'=4,'zl'=2,'yl'=2,'yh'=4,'core'=2] {'zh','zl'}, dimensions={0} | all-to-all | bytes 1048576 | tf_op jit(solution)/shard_map/all_to_all | solution.py:187
  68.6 12.1 %all_to_all.34 = bf16[8,64,256]{2,1,0:T(8,128)(2,1)S(1)} all-to-all(bf16[8,64,256]{2,1,0:T(8,128)(2,1)S(1)} %broadcast_in_dim.6), channel_id=1, replica_groups=mesh['x'=4,'zh'=4,'zl'=2,'yl'=2,'yh'=4,'core'=2] {'zh','zl'}, dimensions={0} | all-to-all | bytes 524288 | tf_op jit(solution)/shard_map/all_to_all | solution.py:189
  80.6 0.1 broadcast_in_dim.15
  80.8 26.3 %all_to_all.35.tiles_ref = bf16[8,512,256]{2,1,0:T(8,128)(2,1)S(1)} all-to-all(bf16[8,512,256]{2,1,0:T(8,128)(2,1)S(1)} %broadcast_in_dim.15), channel_id=1, replica_groups=mesh['x'=4,'zh'=4,'zl'=2,'yl'=2,'yh'=4,'core'=2] {'x','yl'}, dimensions={0} | all-to-all | bytes 4194304 | tf_op jit(solution)/shard_map/all_to_all | solution.py:191
  107.0 8.1 %shard_map.49 = (f32[16,1024]{1,0:T(8,128)}, f32[16,1024]{1,0:T(8,128)}, f32[16,1024]{1,0:T(8,128)S(1)}, f32[128,128]{1,0:T(8,128)S(1)}) custom-call(bf16[8,512,256]{2,1,0:T(8,128)(2,1)S(1)} %all_to_all.35.tiles_ref), custom_call_target="tpu_custom_call" | custom-call | tf_op jit(solution)/shard_map/pallas_call | solution.py:144
  115.1 22.3 %all_to_all.36 = f32[128,1,128]{2,1,0:T(1,128)S(1)} all-to-all(f32[128,1,128]{2,1,0:T(1,128)S(1)} %bitcast.40), channel_id=1, replica_groups=mesh['x'=4,'zh'=4,'zl'=2,'yl'=2,'yh'=4,'core'=2] {'x','zl','yl','yh','co..., dimensions={0} | all-to-all | bytes 131072 | tf_op jit(solution)/shard_map/all_to_all | solution.py:195
  137.4 0.6 slice_reduce_fusion
  138.7 0.6 broadcast_multiply_fusion
  (12 shorter events, 0.3 us)
Async XLA Ops:
  32.3 9.0 %collective-permute-start = (bf16[2048,256]{1,0:T(8,128)(2,1)}, bf16[2048,256]{1,0:T(8,128)(2,1)S(1)}, u32[]{:S(2)}, u32[]{:S(2)}) collective-permute-start(bf16[2048,256]{1,0:T(8,128)(2,1)} %slice.32), channel_id=1, source_target_pairs={{0,1},{1,0},{2,3},{3,2},{4,5},{5,4},{6,7},{7,6},{8,9},{9,8},{10,11... | collective-permute-start | bytes 3145736 | tf_op jit(solution)/shard_map/ppermute | solution.py:182

commit v5 on v4

--- a/solution.py
+++ b/solution.py
@@ -157,8 +157,44 @@
     )(tiles)
 
 
+def cut_kernel(got_ref, mine_ref):
+    mine_ref[...] = got_ref[:, : mine_ref.shape[1]]
+
+
+def cut(got, columns):
+    vmem = pl.BlockSpec(memory_space=pltpu.VMEM)
+    return pl.pallas_call(
+        cut_kernel,
+        out_shape=jax.ShapeDtypeStruct((got.shape[0], columns), LOW),
+        in_specs=[vmem],
+        out_specs=vmem,
+        compiler_params=pltpu.CompilerParams(vmem_limit_bytes=16 * 1024 * 1024),
+    )(got)
+
+
 def against(left, right):
     return lax.dot_general(left, right, (((0,), (0,)), ((), ())), preferred_element_type=F32)
+
+
+def join_kernel(got_ref, other_ref, mine_ref, tile_ref):
+    core = lax.axis_index("core")
+    half = mine_ref.shape[0]
+    tile_ref[pl.ds(pl.multiple_of(core * half, half), half), :] = mine_ref[...]
+    tile_ref[pl.ds(pl.multiple_of((1 - core) * half, half), half), :] = against(
+        other_ref[...], got_ref[:, half:]
+    )
+
+
+def join(got, other, mine):
+    vmem = pl.BlockSpec(memory_space=pltpu.VMEM)
+    rows, columns = mine.shape
+    return pl.pallas_call(
+        join_kernel,
+        out_shape=jax.ShapeDtypeStruct((2 * rows, columns), F32),
+        in_specs=[vmem, vmem, vmem],
+        out_specs=vmem,
+        compiler_params=pltpu.CompilerParams(vmem_limit_bytes=16 * 1024 * 1024),
+    )(got, other, mine)
 
 
 def per_device(acts, up_grad):
@@ -178,12 +214,8 @@
         ]
     )
     got = lax.all_to_all(sent, PLANE, 0, 0, tiled=True).reshape(plane * tokens, 512)
-    mine, cols = got[:, :256], got[:, 256:]
-    other = lax.ppermute(mine, "core", [(0, 1), (1, 0)])
-    mine, other = against(mine, cols), against(other, cols)
-    tile = jnp.where(
-        core == 0, jnp.concatenate([mine, other]), jnp.concatenate([other, mine])
-    ).reshape(depth, 64, 256)
+    other = lax.ppermute(cut(got, 256), "core", [(0, 1), (1, 0)])
+    tile = join(got, other, against(got[:, :256], got[:, 256:])).reshape(depth, 64, 256)
     parts = lax.all_to_all(tile, DEPTH, 0, 0, tiled=True)
     piece = (jnp.sum(parts, axis=0) / (tokens * owners)).astype(LOW)
     tile = lax.all_to_all(jnp.broadcast_to(piece[None], (depth, 64, 256)), DEPTH, 0, 0, tiled=True)
@@ -193,7 +225,7 @@
     )
     left, right, product, total = roots(tiles, rows, 128)
     totals = lax.all_to_all(total, SPREAD, 0, 0, tiled=True)
-    mean = jnp.sum(totals[:, 0]) / (width * width * 8)
+    mean = jnp.sum(totals, axis=0, keepdims=True)[:, :1] / (width * width * 8)
     update = product * lax.rsqrt(mean + 1e-06)
     return (left, right, update)
 

time: 140 us -> 137 us (0.979)
  no operation moved by 1% of the time
where the time goes in v5:
time: 137 us
  blocking collectives  116 us (85%)
  Pallas kernels  8.61 us (6%)
  starting transfers between devices  6.54 us (5%)
  waiting for transfers between devices  1.79 us (1%)
  local copies, waits for them, and re-layouts  1.43 us (1%)
    all_to_all x1, blocking collectives, per_device(): lax.all_to_all(sent, PLANE, 0, 0, tiled=True).reshape(plane * tokens, 512)  29.1 us
    all_to_all x1, blocking collectives, per_device(): parts = lax.all_to_all(tile, DEPTH, 0, 0, tiled=True)  26.6 us
    all_to_all x1, blocking collectives, per_device(): lax.all_to_all(jnp.broadcast_to(tile[None], (plane, 512, 256)), PLANE, 0,...  26.1 us
    all_to_all x1, blocking collectives, per_device(): totals = lax.all_to_all(total, SPREAD, 0, 0, tiled=True)  22.7 us
    all_to_all x1, blocking collectives, per_device(): lax.all_to_all(jnp.broadcast_to(piece[None], (depth, 64, 256)), DEPTH, 0,...  11.9 us
    pallas_call x1, Pallas kernels, roots(): pl.pallas_call(roots_kernel, out_shape=(shape, shape, shape, jax.ShapeDty...  8.06 us
    ppermute x1, starting transfers between devices, per_device(): other = lax.ppermute(cut(got, 256), 'core', [(0, 1), (1, 0)])  6.54 us
  transfers between devices with their start and end apart: 1, of which 1 were waited for; matrix products, arithmetic and copies ran while one was open for 0% of the time, Pallas kernels for 0%

profile of v5, /device:TPU:1, one launch (start us, length us, event | category | flops | bytes accessed | tf_op | source)
XLA Modules:
  0.0 137.1 jit_solution(554606291786901448)
XLA Ops:
  0.6 1.3 constant_dynamic-slice_fusion
  2.1 29.1 %all_to_all.29 = bf16[8,256,512]{2,1,0:T(8,128)(2,1)S(1)} all-to-all(bf16[8,256,512]{2,1,0:T(8,128)(2,1)S(1)} %fusion.10), channel_id=1, replica_groups=mesh['x'=4,'zh'=4,'zl'=2,'yl'=2,'yh'=4,'core'=2] {'x','yl'}, dimensions={0} | all-to-all | bytes 4194304 | tf_op jit(solution)/shard_map/all_to_all | solution.py:216
  31.3 0.1 shard_map.49
  31.3 6.5 %collective-permute-start = (bf16[2048,256]{1,0:T(8,128)(2,1)S(1)}, bf16[2048,256]{1,0:T(8,128)(2,1)S(1)}, u32[]{:S(2)}, u32[]{:S(2)}) collective-permute-start(bf16[2048,256]{1,0:T(8,128)(2,1)S(1)} %shard_map.49), channel_id=1, source_target_pairs={{0,1},{1,0},{2,3},{3,2},{4,5},{5,4},{6,7},{7,6},{8,9},{9,8},{10,11... | collective-permute-start | bytes 3145736 | tf_op jit(solution)/shard_map/ppermute | solution.py:217
  37.9 0.5 fusion.mine_ref
  38.4 1.8 %collective-permute-done.other_ref = bf16[2048,256]{1,0:T(8,128)(2,1)S(1)} collective-permute-done((bf16[2048,256]{1,0:T(8,128)(2,1)S(1)}, bf16[2048,256]{1,0:T(8,128)(2,1)S(1)}, u32[]{:S(2)}, u32[]{:S(2)}) %collective-permute-start) | collective-permute-done | bytes 1048608 | tf_op jit(solution)/shard_map/ppermute | solution.py:217
  40.2 0.5 shard_map.50
  40.6 26.6 %all_to_all.30 = f32[8,64,256]{2,1,0:T(8,128)S(1)} all-to-all(f32[8,64,256]{2,1,0:T(8,128)S(1)} %bitcast.44), channel_id=1, replica_groups=mesh['x'=4,'zh'=4,'zl'=2,'yl'=2,'yh'=4,'core'=2] {'zh','zl'}, dimensions={0} | all-to-all | bytes 1048576 | tf_op jit(solution)/shard_map/all_to_all | solution.py:219
  67.3 11.9 %all_to_all.31 = bf16[8,64,256]{2,1,0:T(8,128)(2,1)S(1)} all-to-all(bf16[8,64,256]{2,1,0:T(8,128)(2,1)S(1)} %broadcast_in_dim.16), channel_id=1, replica_groups=mesh['x'=4,'zh'=4,'zl'=2,'yl'=2,'yh'=4,'core'=2] {'zh','zl'}, dimensions={0} | all-to-all | bytes 524288 | tf_op jit(solution)/shard_map/all_to_all | solution.py:221
  79.2 0.1 broadcast_in_dim.18
  79.4 26.1 %all_to_all.32.tiles_ref = bf16[8,512,256]{2,1,0:T(8,128)(2,1)S(1)} all-to-all(bf16[8,512,256]{2,1,0:T(8,128)(2,1)S(1)} %broadcast_in_dim.18), channel_id=1, replica_groups=mesh['x'=4,'zh'=4,'zl'=2,'yl'=2,'yh'=4,'core'=2] {'x','yl'}, dimensions={0} | all-to-all | bytes 4194304 | tf_op jit(solution)/shard_map/all_to_all | solution.py:223
  105.5 8.1 %shard_map.51 = (f32[16,1024]{1,0:T(8,128)}, f32[16,1024]{1,0:T(8,128)}, f32[16,1024]{1,0:T(8,128)S(1)}, f32[128,128]{1,0:T(8,128)S(1)}) custom-call(bf16[8,512,256]{2,1,0:T(8,128)(2,1)S(1)} %all_to_all.32.tiles_ref), custom_call_target="tpu_custom_call" | custom-call | tf_op jit(solution)/shard_map/pallas_call | solution.py:144
  113.5 22.7 %all_to_all.33 = f32[128,1,128]{2,1,0:T(1,128)S(1)} all-to-all(f32[128,1,128]{2,1,0:T(1,128)S(1)} %bitcast.45), channel_id=1, replica_groups=mesh['x'=4,'zh'=4,'zl'=2,'yl'=2,'yh'=4,'core'=2] {'x','zl','yl','yh','co..., dimensions={0} | all-to-all | bytes 131072 | tf_op jit(solution)/shard_map/all_to_all | solution.py:227
  136.3 0.2 reduce_sum.19
  136.5 0.6 broadcast_multiply_fusion
  (11 shorter events, 0.2 us)
Async XLA Ops:
  31.3 8.8 %collective-permute-start = (bf16[2048,256]{1,0:T(8,128)(2,1)S(1)}, bf16[2048,256]{1,0:T(8,128)(2,1)S(1)}, u32[]{:S(2)}, u32[]{:S(2)}) collective-permute-start(bf16[2048,256]{1,0:T(8,128)(2,1)S(1)} %shard_map.49), channel_id=1, source_target_pairs={{0,1},{1,0},{2,3},{3,2},{4,5},{5,4},{6,7},{7,6},{8,9},{9,8},{10,11... | collective-permute-start | bytes 3145736 | tf_op jit(solution)/shard_map/ppermute | solution.py:217

commit v6 on v5

--- a/solution.py
+++ b/solution.py
@@ -30,21 +30,23 @@
     return both[:rows] + both[rows:]
 
 
-def roots_kernel(
-    tiles_ref, left_ref, right_ref, product_ref, total_ref, grad, stat, rest, turned, keep
-):
+def roots_kernel(mine_ref, other_ref, rows_ref, total_ref, grad, stat, rest, turned, keep):
     width = grad.shape[0]
-    rows = left_ref.shape[0]
-    n_tiles, high, wide = tiles_ref.shape
+    rows = rows_ref.shape[0] // 3
+    n_tiles, high, wide = mine_ref.shape
     groups = keep.shape[0] // rows
     count = groups * rows
-    first = (lax.axis_index("x") * 16 + lax.axis_index("zl") * 2 + lax.axis_index("yl")) * rows
+    core = lax.axis_index("core")
+    first = (lax.axis_index("x") * 16 + core * 2 + lax.axis_index("yl")) * rows
     starts = [pl.multiple_of(first + group * (4 * rows), rows) for group in range(groups)]
     mine = pl.multiple_of(lax.axis_index("zh") * rows, rows)
     start = pl.multiple_of(first + lax.axis_index("zh") * (4 * rows), rows)
     for index in range(n_tiles):
         col, row = index // 2, index % 2
-        grad[row * high : (row + 1) * high, col * wide : (col + 1) * wide] = tiles_ref[index]
+        here = pl.multiple_of((2 * row + core) * high, high)
+        there = pl.multiple_of((2 * row + 1 - core) * high, high)
+        grad[pl.ds(here, high), col * wide : (col + 1) * wide] = mine_ref[index]
+        grad[pl.ds(there, high), col * wide : (col + 1) * wide] = other_ref[index]
 
     side = 256
     on_diagonal = lax.broadcasted_iota(jnp.int32, (side, side), 0) == lax.broadcasted_iota(
@@ -118,7 +120,7 @@
     inner += 0.25 * vector[count:]
     left = 1.5625 * eyes - (0.3125 * power + 0.25 * vector[:count])
     keep[...] = left
-    left_ref[...] = keep[pl.ds(mine, rows), :]
+    rows_ref[:rows, :] = keep[pl.ds(mine, rows), :]
 
     power = times(left, stat[...]) + jnp.dot(
         left.astype(LOW), rest[...], preferred_element_type=F32
@@ -130,22 +132,24 @@
     twice = 1.5625 * left - (0.3125 * power + 0.25 * vector)
     out = times(jnp.concatenate([inner, twice], axis=0), grad[...])
     base = 1.5625 - delta * (0.3125 + 0.25 * (square * square * tau))
-    right_ref[...] = base * eye_of(start) - inverse * out[:rows]
+    rows_ref[rows : 2 * rows, :] = base * eye_of(start) - inverse * out[:rows]
     product = out[rows:]
     total_ref[...] = jnp.full(total_ref.shape, jnp.sum(product * product), F32)
     keep[...] = product
-    product_ref[...] = keep[pl.ds(mine, rows), :]
-
-
-def roots(tiles, rows, devices):
+    rows_ref[2 * rows :, :] = keep[pl.ds(mine, rows), :]
+
+
+def roots(mine, other, rows, devices):
     width = 1024
-    shape = jax.ShapeDtypeStruct((rows, width), F32)
     vmem = pl.BlockSpec(memory_space=pltpu.VMEM)
     return pl.pallas_call(
         roots_kernel,
-        out_shape=(shape, shape, shape, jax.ShapeDtypeStruct((devices, 128), F32)),
-        in_specs=[vmem],
-        out_specs=(vmem, vmem, vmem, vmem),
+        out_shape=(
+            jax.ShapeDtypeStruct((3 * rows, width), F32),
+            jax.ShapeDtypeStruct((devices, 128), F32),
+        ),
+        in_specs=[vmem, vmem],
+        out_specs=(vmem, vmem),
         scratch_shapes=[
             pltpu.VMEM((width, width), LOW),
             pltpu.VMEM((width, width), LOW),
@@ -154,18 +158,18 @@
             pltpu.VMEM((4 * rows, width), F32),
         ],
         compiler_params=pltpu.CompilerParams(vmem_limit_bytes=32 * 1024 * 1024),
-    )(tiles)
-
-
-def cut_kernel(got_ref, mine_ref):
-    mine_ref[...] = got_ref[:, : mine_ref.shape[1]]
-
-
-def cut(got, columns):
+    )(mine, other)
+
+
+def cut_kernel(got_ref, cols_ref):
+    cols_ref[...] = got_ref[:, cols_ref.shape[1] :]
+
+
+def cut(got):
     vmem = pl.BlockSpec(memory_space=pltpu.VMEM)
     return pl.pallas_call(
         cut_kernel,
-        out_shape=jax.ShapeDtypeStruct((got.shape[0], columns), LOW),
+        out_shape=jax.ShapeDtypeStruct((got.shape[0], got.shape[1] // 2), LOW),
         in_specs=[vmem],
         out_specs=vmem,
         compiler_params=pltpu.CompilerParams(vmem_limit_bytes=16 * 1024 * 1024),
@@ -179,18 +183,17 @@
 def join_kernel(got_ref, other_ref, mine_ref, tile_ref):
     core = lax.axis_index("core")
     half = mine_ref.shape[0]
-    tile_ref[pl.ds(pl.multiple_of(core * half, half), half), :] = mine_ref[...]
-    tile_ref[pl.ds(pl.multiple_of((1 - core) * half, half), half), :] = against(
-        other_ref[...], got_ref[:, half:]
-    )
-
-
-def join(got, other, mine):
+    depth, _, rows, columns = tile_ref.shape
+    tile_ref[:, core] = mine_ref[...].reshape(depth, rows, columns)
+    tile_ref[:, 1 - core] = against(got_ref[:, :half], other_ref[...]).reshape(depth, rows, columns)
+
+
+def join(got, other, mine, depth):
     vmem = pl.BlockSpec(memory_space=pltpu.VMEM)
     rows, columns = mine.shape
     return pl.pallas_call(
         join_kernel,
-        out_shape=jax.ShapeDtypeStruct((2 * rows, columns), F32),
+        out_shape=jax.ShapeDtypeStruct((depth // 2, 2, rows * 2 // depth, columns), F32),
         in_specs=[vmem, vmem, vmem],
         out_specs=vmem,
         compiler_params=pltpu.CompilerParams(vmem_limit_bytes=16 * 1024 * 1024),
@@ -214,20 +217,23 @@
         ]
     )
     got = lax.all_to_all(sent, PLANE, 0, 0, tiled=True).reshape(plane * tokens, 512)
-    other = lax.ppermute(cut(got, 256), "core", [(0, 1), (1, 0)])
-    tile = join(got, other, against(got[:, :256], got[:, 256:])).reshape(depth, 64, 256)
-    parts = lax.all_to_all(tile, DEPTH, 0, 0, tiled=True)
+    swap = [(0, 1), (1, 0)]
+    other = lax.ppermute(cut(got), "core", swap)
+    tile = join(got, other, against(got[:, :256], got[:, 256:]), depth)
+    parts = lax.all_to_all(tile.reshape(depth, 64, 256), DEPTH, 0, 0, tiled=True)
     piece = (jnp.sum(parts, axis=0) / (tokens * owners)).astype(LOW)
-    tile = lax.all_to_all(jnp.broadcast_to(piece[None], (depth, 64, 256)), DEPTH, 0, 0, tiled=True)
-    tile = tile.reshape(512, 256)
-    tiles = lax.all_to_all(
-        jnp.broadcast_to(tile[None], (plane, 512, 256)), PLANE, 0, 0, tiled=True
-    )
-    left, right, product, total = roots(tiles, rows, 128)
+    pieces = jnp.broadcast_to(piece[None], (depth // 2, 64, 256))
+    tile = lax.all_to_all(pieces, "zh", 0, 0, tiled=True).reshape(256, 256)
+    mine = lax.all_to_all(
+        jnp.broadcast_to(tile[None], (plane, 256, 256)), PLANE, 0, 0, tiled=True
+    )
+    other = lax.ppermute(mine, "core", swap)
+    found, total = roots(mine, other, rows, 128)
+    found = lax.ppermute(found, ("zl", "core"), [(0, 0), (1, 2), (2, 1), (3, 3)])
     totals = lax.all_to_all(total, SPREAD, 0, 0, tiled=True)
     mean = jnp.sum(totals, axis=0, keepdims=True)[:, :1] / (width * width * 8)
-    update = product * lax.rsqrt(mean + 1e-06)
-    return (left, right, update)
+    update = found[2 * rows :] * lax.rsqrt(mean + 1e-06)
+    return (found[:rows], found[rows : 2 * rows], update)
 
 
 def solution(mesh):

time: 137 us -> 131 us (0.956)
  blocking collectives: 116 us -> 100 us
  starting transfers between devices: 6.54 us -> 14.6 us
  waiting for transfers between devices: 1.79 us -> 4.06 us
    all_to_all x3, blocking collectives: 64.6 us -> 51.1 us  [the longest x1 26.6 us: per_device(): lax.all_to_all(tile.reshape(depth, 64, 256), DEPTH, 0, 0, tiled=True)]
    ppermute x1 -> x3, starting transfers between devices: 6.54 us -> 14.6 us  [the longest x1 6.54 us: per_device(): other = lax.ppermute(cut(got), 'core', swap)]
    all_to_all x1, blocking collectives: 22.7 us -> 20 us  [per_device(): totals = lax.all_to_all(total, SPREAD, 0, 0, tiled=True)]
    ppermute x1 -> x3, waiting for transfers between devices: 1.79 us -> 4.06 us  [the longest x1 2.26 us: per_device(): other = lax.ppermute(mine, 'core', swap)]
  transfers between devices with their start and end apart: 1 -> 3, of which waited for: 1 -> 2; matrix products, arithmetic and copies ran while one was open for 0% -> 0% of each run, Pallas kernels for 0% -> 0%
where the time goes in v6:
time: 131 us
  blocking collectives  100 us (76%)
  starting transfers between devices  14.6 us (11%)
  Pallas kernels  8.33 us (6%)
  waiting for transfers between devices  4.06 us (3%)
  local copies, waits for them, and re-layouts  1.35 us (1%)
    all_to_all x1, blocking collectives, per_device(): lax.all_to_all(sent, PLANE, 0, 0, tiled=True).reshape(plane * tokens, 512)  29.1 us
    all_to_all x1, blocking collectives, per_device(): lax.all_to_all(tile.reshape(depth, 64, 256), DEPTH, 0, 0, tiled=True)  26.6 us
    all_to_all x1, blocking collectives, per_device(): totals = lax.all_to_all(total, SPREAD, 0, 0, tiled=True)  20 us
    all_to_all x1, blocking collectives, per_device(): lax.all_to_all(jnp.broadcast_to(tile[None], (plane, 256, 256)), PLANE, 0,...  14.9 us
    all_to_all x1, blocking collectives, per_device(): tile = lax.all_to_all(pieces, 'zh', 0, 0, tiled=True).reshape(256, 256)  9.64 us
    pallas_call x1, Pallas kernels, roots(): pl.pallas_call(roots_kernel, out_shape=(jax.ShapeDtypeStruct((3 * rows, w...  7.78 us
    ppermute x1, starting transfers between devices, per_device(): other = lax.ppermute(cut(got), 'core', swap)  6.54 us
    ppermute x1, starting transfers between devices, per_device(): other = lax.ppermute(mine, 'core', swap)  6.09 us
  transfers between devices with their start and end apart: 3, of which 2 were waited for; matrix products, arithmetic and copies ran while one was open for 0% of the time, Pallas kernels for 0%

profile of v6, /device:TPU:1, one launch (start us, length us, event | category | flops | bytes accessed | tf_op | source)
XLA Modules:
  0.0 130.9 jit_solution(12608614650502159658)
XLA Ops:
  0.6 1.3 constant_dynamic-slice_fusion
  2.1 29.1 %all_to_all.29 = bf16[8,256,512]{2,1,0:T(8,128)(2,1)S(1)} all-to-all(bf16[8,256,512]{2,1,0:T(8,128)(2,1)S(1)} %fusion.10), channel_id=1, replica_groups=mesh['x'=4,'zh'=4,'zl'=2,'yl'=2,'yh'=4,'core'=2] {'x','yl'}, dimensions={0} | all-to-all | bytes 4194304 | tf_op jit(solution)/shard_map/all_to_all | solution.py:219
  31.3 0.1 shard_map.49
  31.3 6.5 %collective-permute-start = (bf16[2048,256]{1,0:T(8,128)(2,1)S(1)}, bf16[2048,256]{1,0:T(8,128)(2,1)S(1)}, u32[]{:S(2)}, u32[]{:S(2)}) collective-permute-start(bf16[2048,256]{1,0:T(8,128)(2,1)S(1)} %shard_map.49), channel_id=1, source_target_pairs={{0,1},{1,0},{2,3},{3,2},{4,5},{5,4},{6,7},{7,6},{8,9},{9,8},{10,11... | collective-permute-start | bytes 3145736 | tf_op jit(solution)/shard_map/ppermute | solution.py:221
  37.9 0.5 fusion.mine_ref
  38.4 1.8 %collective-permute-done.other_ref = bf16[2048,256]{1,0:T(8,128)(2,1)S(1)} collective-permute-done((bf16[2048,256]{1,0:T(8,128)(2,1)S(1)}, bf16[2048,256]{1,0:T(8,128)(2,1)S(1)}, u32[]{:S(2)}, u32[]{:S(2)}) %collective-permute-start) | collective-permute-done | bytes 1048608 | tf_op jit(solution)/shard_map/ppermute | solution.py:221
  40.2 0.5 shard_map.50
  40.6 26.6 %all_to_all.30 = f32[8,64,256]{2,1,0:T(8,128)S(1)} all-to-all(f32[8,64,256]{2,1,0:T(8,128)S(1)} %bitcast.44), channel_id=1, replica_groups=mesh['x'=4,'zh'=4,'zl'=2,'yl'=2,'yh'=4,'core'=2] {'zh','zl'}, dimensions={0} | all-to-all | bytes 1048576 | tf_op jit(solution)/shard_map/all_to_all | solution.py:223
  67.3 9.6 %all_to_all.31 = bf16[4,64,256]{2,1,0:T(8,128)(2,1)S(1)} all-to-all(bf16[4,64,256]{2,1,0:T(8,128)(2,1)S(1)} %broadcast_in_dim.16), channel_id=1, replica_groups=mesh['x'=4,'zh'=4,'zl'=2,'yl'=2,'yh'=4,'core'=2] {'zh'}, dimensions={0} | all-to-all | bytes 262144 | tf_op jit(solution)/shard_map/all_to_all | solution.py:226
  76.9 0.1 broadcast_in_dim.18
  77.0 14.9 %all_to_all.32.mine_ref = bf16[8,256,256]{2,1,0:T(8,128)(2,1)S(1)} all-to-all(bf16[8,256,256]{2,1,0:T(8,128)(2,1)S(1)} %broadcast_in_dim.18), channel_id=1, replica_groups=mesh['x'=4,'zh'=4,'zl'=2,'yl'=2,'yh'=4,'core'=2] {'x','yl'}, dimensions={0} | all-to-all | bytes 2097152 | tf_op jit(solution)/shard_map/all_to_all | solution.py:227
  91.9 6.1 %collective-permute-start.1 = (bf16[8,256,256]{2,1,0:T(8,128)(2,1)S(1)}, bf16[8,256,256]{2,1,0:T(8,128)(2,1)S(1)}, u32[]{:S(2)}, u32[]{:S(2)}) collective-permute-start(bf16[8,256,256]{2,1,0:T(8,128)(2,1)S(1)} %all_to_all.32.mine_ref), channel_id=1, source_target_pairs={{0,1},{1,0},{2,3},{3,2},{4,5},{5,4},{6,7},{7,6},{8,9},{9,8},{10,11... | collective-permute-start | bytes 3145736 | tf_op jit(solution)/shard_map/ppermute | solution.py:230
  98.0 2.3 %collective-permute-done.1.other_ref = bf16[8,256,256]{2,1,0:T(8,128)(2,1)S(1)} collective-permute-done((bf16[8,256,256]{2,1,0:T(8,128)(2,1)S(1)}, bf16[8,256,256]{2,1,0:T(8,128)(2,1)S(1)}, u32[]{:S(2)}, u32[]{:S(2)}) %collective-permute-start.1) | collective-permute-done | bytes 1048608 | tf_op jit(solution)/shard_map/ppermute | solution.py:230
  100.3 7.8 %shard_map.51 = (f32[48,1024]{1,0:T(8,128)S(1)}, f32[128,128]{1,0:T(8,128)S(1)}) custom-call(bf16[8,256,256]{2,1,0:T(8,128)(2,1)S(1)} %all_to_all.32.mine_ref, bf16[8,256,256]{2,1,0:T(8,128)(2,1)S(1)} %collective-permute-done.1.other_ref), custom_call_target="tpu_custom_call" | custom-call | tf_op jit(solution)/shard_map/pallas_call | solution.py:145
  108.0 1.9 %collective-permute-start.2 = (f32[48,1024]{1,0:T(8,128)S(1)}, f32[48,1024]{1,0:T(8,128)S(1)}, u32[]{:S(2)}, u32[]{:S(2)}) collective-permute-start(f32[48,1024]{1,0:T(8,128)S(1)} %get-tuple-element.5), channel_id=1, source_target_pairs={{0,0},{1,16},{16,1},{17,17},{2,2},{3,18},{18,3},{19,19},{4,4},{5,2... | collective-permute-start | bytes 589832 | tf_op jit(solution)/shard_map/ppermute | solution.py:232
  110.0 20.0 %all_to_all.33 = f32[128,1,128]{2,1,0:T(1,128)S(1)} all-to-all(f32[128,1,128]{2,1,0:T(1,128)S(1)} %bitcast.45), channel_id=1, replica_groups=mesh['x'=4,'zh'=4,'zl'=2,'yl'=2,'yh'=4,'core'=2] {'x','zl','yl','yh','co..., dimensions={0} | all-to-all | bytes 131072 | tf_op jit(solution)/shard_map/all_to_all | solution.py:233
  130.0 0.2 reduce_sum.19
  130.2 0.0 collective-permute-done.2
  130.2 0.7 slice_multiply_fusion
  (11 shorter events, 0.2 us)
Async XLA Ops:
  31.3 8.8 %collective-permute-start = (bf16[2048,256]{1,0:T(8,128)(2,1)S(1)}, bf16[2048,256]{1,0:T(8,128)(2,1)S(1)}, u32[]{:S(2)}, u32[]{:S(2)}) collective-permute-start(bf16[2048,256]{1,0:T(8,128)(2,1)S(1)} %shard_map.49), channel_id=1, source_target_pairs={{0,1},{1,0},{2,3},{3,2},{4,5},{5,4},{6,7},{7,6},{8,9},{9,8},{10,11... | collective-permute-start | bytes 3145736 | tf_op jit(solution)/shard_map/ppermute | solution.py:221
  91.9 8.4 %collective-permute-start.1 = (bf16[8,256,256]{2,1,0:T(8,128)(2,1)S(1)}, bf16[8,256,256]{2,1,0:T(8,128)(2,1)S(1)}, u32[]{:S(2)}, u32[]{:S(2)}) collective-permute-start(bf16[8,256,256]{2,1,0:T(8,128)(2,1)S(1)} %all_to_all.32.mine_ref), channel_id=1, source_target_pairs={{0,1},{1,0},{2,3},{3,2},{4,5},{5,4},{6,7},{7,6},{8,9},{9,8},{10,11... | collective-permute-start | bytes 3145736 | tf_op jit(solution)/shard_map/ppermute | solution.py:230
  108.0 22.2 %collective-permute-start.2 = (f32[48,1024]{1,0:T(8,128)S(1)}, f32[48,1024]{1,0:T(8,128)S(1)}, u32[]{:S(2)}, u32[]{:S(2)}) collective-permute-start(f32[48,1024]{1,0:T(8,128)S(1)} %get-tuple-element.5), channel_id=1, source_target_pairs={{0,0},{1,16},{16,1},{17,17},{2,2},{3,18},{18,3},{19,19},{4,4},{5,2... | collective-permute-start | bytes 589832 | tf_op jit(solution)/shard_map/ppermute | solution.py:232

commit v7 on v6

--- a/solution.py
+++ b/solution.py
@@ -12,7 +12,7 @@
 TENSOR = ("yh", "core")
 PLANE = ("x", "yl")
 DEPTH = ("zh", "zl")
-SPREAD = ("x", "zl", "yl", "yh", "core")
+SPREAD = ("core", "zl", "yl", "x", "yh")
 F32 = jnp.float32
 LOW = jnp.bfloat16
 ACROSS = (((1,), (1,)), ((), ()))
@@ -162,14 +162,16 @@
 
 
 def cut_kernel(got_ref, cols_ref):
-    cols_ref[...] = got_ref[:, cols_ref.shape[1] :]
+    half = cols_ref.shape[1]
+    cols_ref[...] = got_ref[:, half:, :].reshape(cols_ref.shape)
 
 
 def cut(got):
     vmem = pl.BlockSpec(memory_space=pltpu.VMEM)
+    senders, both, columns = got.shape
     return pl.pallas_call(
         cut_kernel,
-        out_shape=jax.ShapeDtypeStruct((got.shape[0], got.shape[1] // 2), LOW),
+        out_shape=jax.ShapeDtypeStruct((senders * both // 2, columns), LOW),
         in_specs=[vmem],
         out_specs=vmem,
         compiler_params=pltpu.CompilerParams(vmem_limit_bytes=16 * 1024 * 1024),
@@ -180,12 +182,33 @@
     return lax.dot_general(left, right, (((0,), (0,)), ((), ())), preferred_element_type=F32)
 
 
+def own_kernel(got_ref, mine_ref):
+    half, columns = mine_ref.shape
+    left = got_ref[:, :half, :].reshape(-1, columns)
+    right = got_ref[:, half:, :].reshape(-1, columns)
+    mine_ref[...] = against(left, right)
+
+
+def own(got):
+    vmem = pl.BlockSpec(memory_space=pltpu.VMEM)
+    _, both, columns = got.shape
+    return pl.pallas_call(
+        own_kernel,
+        out_shape=jax.ShapeDtypeStruct((both // 2, columns), F32),
+        in_specs=[vmem],
+        out_specs=vmem,
+        compiler_params=pltpu.CompilerParams(vmem_limit_bytes=16 * 1024 * 1024),
+        cost_estimate=pl.CostEstimate(flops=2**28, bytes_accessed=2**21, transcendentals=0),
+    )(got)
+
+
 def join_kernel(got_ref, other_ref, mine_ref, tile_ref):
     core = lax.axis_index("core")
     half = mine_ref.shape[0]
     depth, _, rows, columns = tile_ref.shape
+    left = got_ref[:, :half, :].reshape(-1, columns)
     tile_ref[:, core] = mine_ref[...].reshape(depth, rows, columns)
-    tile_ref[:, 1 - core] = against(got_ref[:, :half], other_ref[...]).reshape(depth, rows, columns)
+    tile_ref[:, 1 - core] = against(left, other_ref[...]).reshape(depth, rows, columns)
 
 
 def join(got, other, mine, depth):
@@ -212,14 +235,14 @@
     ]
     sent = jnp.stack(
         [
-            jnp.concatenate([halves[i % 2], up_grad[:, i // 2 * 256 : i // 2 * 256 + 256]], axis=1)
+            jnp.concatenate([halves[i % 2], up_grad[:, i // 2 * 256 : i // 2 * 256 + 256]], axis=0)
             for i in range(plane)
         ]
     )
-    got = lax.all_to_all(sent, PLANE, 0, 0, tiled=True).reshape(plane * tokens, 512)
+    got = lax.all_to_all(sent, PLANE, 0, 0, tiled=True)
     swap = [(0, 1), (1, 0)]
     other = lax.ppermute(cut(got), "core", swap)
-    tile = join(got, other, against(got[:, :256], got[:, 256:]), depth)
+    tile = join(got, other, own(got), depth)
     parts = lax.all_to_all(tile.reshape(depth, 64, 256), DEPTH, 0, 0, tiled=True)
     piece = (jnp.sum(parts, axis=0) / (tokens * owners)).astype(LOW)
     pieces = jnp.broadcast_to(piece[None], (depth // 2, 64, 256))

time: 131 us -> 131 us (level)
  no operation moved by 1% of the time
where the time goes in v7:
time: 131 us
  blocking collectives  99.9 us (76%)
  starting transfers between devices  14.6 us (11%)
  Pallas kernels  8.81 us (7%)
  waiting for transfers between devices  4.04 us (3%)
  local copies, waits for them, and re-layouts  1.35 us (1%)
    all_to_all x1, blocking collectives, per_device(): got = lax.all_to_all(sent, PLANE, 0, 0, tiled=True)  29.1 us
    all_to_all x1, blocking collectives, per_device(): lax.all_to_all(tile.reshape(depth, 64, 256), DEPTH, 0, 0, tiled=True)  26.6 us
    all_to_all x1, blocking collectives, per_device(): totals = lax.all_to_all(total, SPREAD, 0, 0, tiled=True)  19.7 us
    all_to_all x1, blocking collectives, per_device(): lax.all_to_all(jnp.broadcast_to(tile[None], (plane, 256, 256)), PLANE, 0,...  14.9 us
    all_to_all x1, blocking collectives, per_device(): tile = lax.all_to_all(pieces, 'zh', 0, 0, tiled=True).reshape(256, 256)  9.64 us
    pallas_call x1, Pallas kernels, roots(): pl.pallas_call(roots_kernel, out_shape=(jax.ShapeDtypeStruct((3 * rows, w...  7.78 us
    ppermute x1, starting transfers between devices, per_device(): other = lax.ppermute(cut(got), 'core', swap)  6.54 us
    ppermute x1, starting transfers between devices, per_device(): other = lax.ppermute(mine, 'core', swap)  6.09 us
  transfers between devices with their start and end apart: 3, of which 2 were waited for; matrix products, arithmetic and copies ran while one was open for 0% of the time, Pallas kernels for 0%

profile of v7, /device:TPU:1, one launch (start us, length us, event | category | flops | bytes accessed | tf_op | source)
XLA Modules:
  0.0 130.6 jit_solution(12309306299962161686)
XLA Ops:
  0.6 1.3 constant_dynamic-slice_fusion
  2.1 29.1 %all_to_all.29.got_ref = bf16[8,512,256]{2,1,0:T(8,128)(2,1)S(1)} all-to-all(bf16[8,512,256]{2,1,0:T(8,128)(2,1)S(1)} %fusion.7), channel_id=1, replica_groups=mesh['x'=4,'zh'=4,'zl'=2,'yl'=2,'yh'=4,'core'=2] {'x','yl'}, dimensions={0} | all-to-all | bytes 4194304 | tf_op jit(solution)/shard_map/all_to_all | solution.py:242
  31.3 0.1 shard_map.49
  31.3 6.5 %collective-permute-start = (bf16[2048,256]{1,0:T(8,128)(2,1)S(1)}, bf16[2048,256]{1,0:T(8,128)(2,1)S(1)}, u32[]{:S(2)}, u32[]{:S(2)}) collective-permute-start(bf16[2048,256]{1,0:T(8,128)(2,1)S(1)} %shard_map.49), channel_id=1, source_target_pairs={{0,1},{1,0},{2,3},{3,2},{4,5},{5,4},{6,7},{7,6},{8,9},{9,8},{10,11... | collective-permute-start | bytes 3145736 | tf_op jit(solution)/shard_map/ppermute | solution.py:244
  37.9 0.5 shard_map.50.mine_ref
  38.4 1.8 %collective-permute-done.other_ref = bf16[2048,256]{1,0:T(8,128)(2,1)S(1)} collective-permute-done((bf16[2048,256]{1,0:T(8,128)(2,1)S(1)}, bf16[2048,256]{1,0:T(8,128)(2,1)S(1)}, u32[]{:S(2)}, u32[]{:S(2)}) %collective-permute-start) | collective-permute-done | bytes 1048608 | tf_op jit(solution)/shard_map/ppermute | solution.py:244
  40.2 0.5 shard_map.51
  40.6 26.6 %all_to_all.30 = f32[8,64,256]{2,1,0:T(8,128)S(1)} all-to-all(f32[8,64,256]{2,1,0:T(8,128)S(1)} %bitcast.40), channel_id=1, replica_groups=mesh['x'=4,'zh'=4,'zl'=2,'yl'=2,'yh'=4,'core'=2] {'zh','zl'}, dimensions={0} | all-to-all | bytes 1048576 | tf_op jit(solution)/shard_map/all_to_all | solution.py:246
  67.3 9.6 %all_to_all.31 = bf16[4,64,256]{2,1,0:T(8,128)(2,1)S(1)} all-to-all(bf16[4,64,256]{2,1,0:T(8,128)(2,1)S(1)} %broadcast_in_dim.16), channel_id=1, replica_groups=mesh['x'=4,'zh'=4,'zl'=2,'yl'=2,'yh'=4,'core'=2] {'zh'}, dimensions={0} | all-to-all | bytes 262144 | tf_op jit(solution)/shard_map/all_to_all | solution.py:249
  76.9 0.1 broadcast_in_dim.18
  77.0 14.9 %all_to_all.32.mine_ref = bf16[8,256,256]{2,1,0:T(8,128)(2,1)S(1)} all-to-all(bf16[8,256,256]{2,1,0:T(8,128)(2,1)S(1)} %broadcast_in_dim.18), channel_id=1, replica_groups=mesh['x'=4,'zh'=4,'zl'=2,'yl'=2,'yh'=4,'core'=2] {'x','yl'}, dimensions={0} | all-to-all | bytes 2097152 | tf_op jit(solution)/shard_map/all_to_all | solution.py:250
  91.9 6.1 %collective-permute-start.1 = (bf16[8,256,256]{2,1,0:T(8,128)(2,1)S(1)}, bf16[8,256,256]{2,1,0:T(8,128)(2,1)S(1)}, u32[]{:S(2)}, u32[]{:S(2)}) collective-permute-start(bf16[8,256,256]{2,1,0:T(8,128)(2,1)S(1)} %all_to_all.32.mine_ref), channel_id=1, source_target_pairs={{0,1},{1,0},{2,3},{3,2},{4,5},{5,4},{6,7},{7,6},{8,9},{9,8},{10,11... | collective-permute-start | bytes 3145736 | tf_op jit(solution)/shard_map/ppermute | solution.py:253
  98.0 2.3 %collective-permute-done.1.other_ref = bf16[8,256,256]{2,1,0:T(8,128)(2,1)S(1)} collective-permute-done((bf16[8,256,256]{2,1,0:T(8,128)(2,1)S(1)}, bf16[8,256,256]{2,1,0:T(8,128)(2,1)S(1)}, u32[]{:S(2)}, u32[]{:S(2)}) %collective-permute-start.1) | collective-permute-done | bytes 1048608 | tf_op jit(solution)/shard_map/ppermute | solution.py:253
  100.3 7.8 %shard_map.52 = (f32[48,1024]{1,0:T(8,128)S(1)}, f32[128,128]{1,0:T(8,128)S(1)}) custom-call(bf16[8,256,256]{2,1,0:T(8,128)(2,1)S(1)} %all_to_all.32.mine_ref, bf16[8,256,256]{2,1,0:T(8,128)(2,1)S(1)} %collective-permute-done.1.other_ref), custom_call_target="tpu_custom_call" | custom-call | tf_op jit(solution)/shard_map/pallas_call | solution.py:145
  108.0 1.9 %collective-permute-start.2 = (f32[48,1024]{1,0:T(8,128)S(1)}, f32[48,1024]{1,0:T(8,128)S(1)}, u32[]{:S(2)}, u32[]{:S(2)}) collective-permute-start(f32[48,1024]{1,0:T(8,128)S(1)} %get-tuple-element.5), channel_id=1, source_target_pairs={{0,0},{1,16},{16,1},{17,17},{2,2},{3,18},{18,3},{19,19},{4,4},{5,2... | collective-permute-start | bytes 589832 | tf_op jit(solution)/shard_map/ppermute | solution.py:255
  110.0 19.7 %all_to_all.33 = f32[128,1,128]{2,1,0:T(1,128)S(1)} all-to-all(f32[128,1,128]{2,1,0:T(1,128)S(1)} %bitcast.41), channel_id=1, replica_groups=mesh['x'=4,'zh'=4,'zl'=2,'yl'=2,'yh'=4,'core'=2] {'core','zl','yl','x','..., dimensions={0} | all-to-all | bytes 131072 | tf_op jit(solution)/shard_map/all_to_all | solution.py:256
  129.6 0.2 reduce_sum.19
  129.9 0.0 collective-permute-done.2
  129.9 0.7 slice_multiply_fusion
  (11 shorter events, 0.2 us)
Async XLA Ops:
  31.3 8.8 %collective-permute-start = (bf16[2048,256]{1,0:T(8,128)(2,1)S(1)}, bf16[2048,256]{1,0:T(8,128)(2,1)S(1)}, u32[]{:S(2)}, u32[]{:S(2)}) collective-permute-start(bf16[2048,256]{1,0:T(8,128)(2,1)S(1)} %shard_map.49), channel_id=1, source_target_pairs={{0,1},{1,0},{2,3},{3,2},{4,5},{5,4},{6,7},{7,6},{8,9},{9,8},{10,11... | collective-permute-start | bytes 3145736 | tf_op jit(solution)/shard_map/ppermute | solution.py:244
  91.9 8.4 %collective-permute-start.1 = (bf16[8,256,256]{2,1,0:T(8,128)(2,1)S(1)}, bf16[8,256,256]{2,1,0:T(8,128)(2,1)S(1)}, u32[]{:S(2)}, u32[]{:S(2)}) collective-permute-start(bf16[8,256,256]{2,1,0:T(8,128)(2,1)S(1)} %all_to_all.32.mine_ref), channel_id=1, source_target_pairs={{0,1},{1,0},{2,3},{3,2},{4,5},{5,4},{6,7},{7,6},{8,9},{9,8},{10,11... | collective-permute-start | bytes 3145736 | tf_op jit(solution)/shard_map/ppermute | solution.py:253
  108.0 21.8 %collective-permute-start.2 = (f32[48,1024]{1,0:T(8,128)S(1)}, f32[48,1024]{1,0:T(8,128)S(1)}, u32[]{:S(2)}, u32[]{:S(2)}) collective-permute-start(f32[48,1024]{1,0:T(8,128)S(1)} %get-tuple-element.5), channel_id=1, source_target_pairs={{0,0},{1,16},{16,1},{17,17},{2,2},{3,18},{18,3},{19,19},{4,4},{5,2... | collective-permute-start | bytes 589832 | tf_op jit(solution)/shard_map/ppermute | solution.py:255

commit v8 on v7

--- a/solution.py
+++ b/solution.py
@@ -11,7 +11,7 @@
 DP = ("x", "zh", "zl", "yl")
 TENSOR = ("yh", "core")
 PLANE = ("x", "yl")
-DEPTH = ("zh", "zl")
+DEPTH = ("zl", "zh")
 SPREAD = ("core", "zl", "yl", "x", "yh")
 F32 = jnp.float32
 LOW = jnp.bfloat16
@@ -205,10 +205,10 @@
 def join_kernel(got_ref, other_ref, mine_ref, tile_ref):
     core = lax.axis_index("core")
     half = mine_ref.shape[0]
-    depth, _, rows, columns = tile_ref.shape
+    _, depth, rows, columns = tile_ref.shape
     left = got_ref[:, :half, :].reshape(-1, columns)
-    tile_ref[:, core] = mine_ref[...].reshape(depth, rows, columns)
-    tile_ref[:, 1 - core] = against(left, other_ref[...]).reshape(depth, rows, columns)
+    tile_ref[core] = mine_ref[...].reshape(depth, rows, columns)
+    tile_ref[1 - core] = against(left, other_ref[...]).reshape(depth, rows, columns)
 
 
 def join(got, other, mine, depth):
@@ -216,7 +216,7 @@
     rows, columns = mine.shape
     return pl.pallas_call(
         join_kernel,
-        out_shape=jax.ShapeDtypeStruct((depth // 2, 2, rows * 2 // depth, columns), F32),
+        out_shape=jax.ShapeDtypeStruct((2, depth // 2, rows * 2 // depth, columns), F32),
         in_specs=[vmem, vmem, vmem],
         out_specs=vmem,
         compiler_params=pltpu.CompilerParams(vmem_limit_bytes=16 * 1024 * 1024),

time: 131 us -> 130 us (level)
  blocking collectives: 99.9 us -> 96.3 us
  starting transfers between devices: 14.6 us -> 17.7 us
    all_to_all x1, blocking collectives: 26.6 us -> 22.7 us  [per_device(): lax.all_to_all(tile.reshape(depth, 64, 256), DEPTH, 0, 0, tiled=True)]
    all_to_all x1, blocking collectives: 9.64 us -> 12.2 us  [per_device(): tile = lax.all_to_all(pieces, 'zh', 0, 0, tiled=True).reshape(256, 256)]
    ppermute x1, starting transfers between devices: 1.92 us -> 4.19 us  [per_device(): lax.ppermute(found, ('zl', 'core'), [(0, 0), (1, 2), (2, 1), (3, 3)])]
    all_to_all x1, blocking collectives: 19.7 us -> 18.1 us  [per_device(): totals = lax.all_to_all(total, SPREAD, 0, 0, tiled=True)]
where the time goes in v8:
time: 130 us
  blocking collectives  96.3 us (74%)
  starting transfers between devices  17.7 us (14%)
  Pallas kernels  8.81 us (7%)
  waiting for transfers between devices  4.04 us (3%)
  local copies, waits for them, and re-layouts  1.35 us (1%)
    all_to_all x1, blocking collectives, per_device(): got = lax.all_to_all(sent, PLANE, 0, 0, tiled=True)  29.1 us
    all_to_all x1, blocking collectives, per_device(): lax.all_to_all(tile.reshape(depth, 64, 256), DEPTH, 0, 0, tiled=True)  22.7 us
    all_to_all x1, blocking collectives, per_device(): totals = lax.all_to_all(total, SPREAD, 0, 0, tiled=True)  18.1 us
    all_to_all x1, blocking collectives, per_device(): lax.all_to_all(jnp.broadcast_to(tile[None], (plane, 256, 256)), PLANE, 0,...  14 us
    all_to_all x1, blocking collectives, per_device(): tile = lax.all_to_all(pieces, 'zh', 0, 0, tiled=True).reshape(256, 256)  12.2 us
    pallas_call x1, Pallas kernels, roots(): pl.pallas_call(roots_kernel, out_shape=(jax.ShapeDtypeStruct((3 * rows, w...  7.78 us
    ppermute x1, starting transfers between devices, per_device(): other = lax.ppermute(mine, 'core', swap)  6.93 us
    ppermute x1, starting transfers between devices, per_device(): other = lax.ppermute(cut(got), 'core', swap)  6.54 us
  transfers between devices with their start and end apart: 3, of which 2 were waited for; matrix products, arithmetic and copies ran while one was open for 0% of the time, Pallas kernels for 0%

profile of v8, /device:TPU:1, one launch (start us, length us, event | category | flops | bytes accessed | tf_op | source)
XLA Modules:
  0.0 130.1 jit_solution(12102213401693829404)
XLA Ops:
  0.6 1.3 constant_dynamic-slice_fusion
  2.1 29.1 %all_to_all.29.got_ref = bf16[8,512,256]{2,1,0:T(8,128)(2,1)S(1)} all-to-all(bf16[8,512,256]{2,1,0:T(8,128)(2,1)S(1)} %fusion.7), channel_id=1, replica_groups=mesh['x'=4,'zh'=4,'zl'=2,'yl'=2,'yh'=4,'core'=2] {'x','yl'}, dimensions={0} | all-to-all | bytes 4194304 | tf_op jit(solution)/shard_map/all_to_all | solution.py:242
  31.3 0.1 shard_map.49
  31.3 6.5 %collective-permute-start = (bf16[2048,256]{1,0:T(8,128)(2,1)S(1)}, bf16[2048,256]{1,0:T(8,128)(2,1)S(1)}, u32[]{:S(2)}, u32[]{:S(2)}) collective-permute-start(bf16[2048,256]{1,0:T(8,128)(2,1)S(1)} %shard_map.49), channel_id=1, source_target_pairs={{0,1},{1,0},{2,3},{3,2},{4,5},{5,4},{6,7},{7,6},{8,9},{9,8},{10,11... | collective-permute-start | bytes 3145736 | tf_op jit(solution)/shard_map/ppermute | solution.py:244
  37.9 0.5 shard_map.50.mine_ref
  38.4 1.8 %collective-permute-done.other_ref = bf16[2048,256]{1,0:T(8,128)(2,1)S(1)} collective-permute-done((bf16[2048,256]{1,0:T(8,128)(2,1)S(1)}, bf16[2048,256]{1,0:T(8,128)(2,1)S(1)}, u32[]{:S(2)}, u32[]{:S(2)}) %collective-permute-start) | collective-permute-done | bytes 1048608 | tf_op jit(solution)/shard_map/ppermute | solution.py:244
  40.2 0.5 shard_map.51
  40.6 22.7 %all_to_all.30 = f32[8,64,256]{2,1,0:T(8,128)S(1)} all-to-all(f32[8,64,256]{2,1,0:T(8,128)S(1)} %bitcast.40), channel_id=1, replica_groups=mesh['x'=4,'zh'=4,'zl'=2,'yl'=2,'yh'=4,'core'=2] {'zl','zh'}, dimensions={0} | all-to-all | bytes 1048576 | tf_op jit(solution)/shard_map/all_to_all | solution.py:246
  63.4 12.2 %all_to_all.31 = bf16[4,64,256]{2,1,0:T(8,128)(2,1)S(1)} all-to-all(bf16[4,64,256]{2,1,0:T(8,128)(2,1)S(1)} %broadcast_in_dim.16), channel_id=1, replica_groups=mesh['x'=4,'zh'=4,'zl'=2,'yl'=2,'yh'=4,'core'=2] {'zh'}, dimensions={0} | all-to-all | bytes 262144 | tf_op jit(solution)/shard_map/all_to_all | solution.py:249
  75.7 0.1 broadcast_in_dim.18
  75.8 14.0 %all_to_all.32.mine_ref = bf16[8,256,256]{2,1,0:T(8,128)(2,1)S(1)} all-to-all(bf16[8,256,256]{2,1,0:T(8,128)(2,1)S(1)} %broadcast_in_dim.18), channel_id=1, replica_groups=mesh['x'=4,'zh'=4,'zl'=2,'yl'=2,'yh'=4,'core'=2] {'x','yl'}, dimensions={0} | all-to-all | bytes 2097152 | tf_op jit(solution)/shard_map/all_to_all | solution.py:250
  89.8 6.9 %collective-permute-start.1 = (bf16[8,256,256]{2,1,0:T(8,128)(2,1)S(1)}, bf16[8,256,256]{2,1,0:T(8,128)(2,1)S(1)}, u32[]{:S(2)}, u32[]{:S(2)}) collective-permute-start(bf16[8,256,256]{2,1,0:T(8,128)(2,1)S(1)} %all_to_all.32.mine_ref), channel_id=1, source_target_pairs={{0,1},{1,0},{2,3},{3,2},{4,5},{5,4},{6,7},{7,6},{8,9},{9,8},{10,11... | collective-permute-start | bytes 3145736 | tf_op jit(solution)/shard_map/ppermute | solution.py:253
  96.7 2.3 %collective-permute-done.1.other_ref = bf16[8,256,256]{2,1,0:T(8,128)(2,1)S(1)} collective-permute-done((bf16[8,256,256]{2,1,0:T(8,128)(2,1)S(1)}, bf16[8,256,256]{2,1,0:T(8,128)(2,1)S(1)}, u32[]{:S(2)}, u32[]{:S(2)}) %collective-permute-start.1) | collective-permute-done | bytes 1048608 | tf_op jit(solution)/shard_map/ppermute | solution.py:253
  99.0 7.8 %shard_map.52 = (f32[48,1024]{1,0:T(8,128)S(1)}, f32[128,128]{1,0:T(8,128)S(1)}) custom-call(bf16[8,256,256]{2,1,0:T(8,128)(2,1)S(1)} %all_to_all.32.mine_ref, bf16[8,256,256]{2,1,0:T(8,128)(2,1)S(1)} %collective-permute-done.1.other_ref), custom_call_target="tpu_custom_call" | custom-call | tf_op jit(solution)/shard_map/pallas_call | solution.py:145
  106.8 4.2 %collective-permute-start.2 = (f32[48,1024]{1,0:T(8,128)S(1)}, f32[48,1024]{1,0:T(8,128)S(1)}, u32[]{:S(2)}, u32[]{:S(2)}) collective-permute-start(f32[48,1024]{1,0:T(8,128)S(1)} %get-tuple-element.5), channel_id=1, source_target_pairs={{0,0},{1,16},{16,1},{17,17},{2,2},{3,18},{18,3},{19,19},{4,4},{5,2... | collective-permute-start | bytes 589832 | tf_op jit(solution)/shard_map/ppermute | solution.py:255
  111.0 18.1 %all_to_all.33 = f32[128,1,128]{2,1,0:T(1,128)S(1)} all-to-all(f32[128,1,128]{2,1,0:T(1,128)S(1)} %bitcast.41), channel_id=1, replica_groups=mesh['x'=4,'zh'=4,'zl'=2,'yl'=2,'yh'=4,'core'=2] {'core','zl','yl','x','..., dimensions={0} | all-to-all | bytes 131072 | tf_op jit(solution)/shard_map/all_to_all | solution.py:256
  129.1 0.2 reduce_sum.19
  129.4 0.0 collective-permute-done.2
  129.4 0.7 slice_multiply_fusion
  (11 shorter events, 0.2 us)
Async XLA Ops:
  31.3 8.8 %collective-permute-start = (bf16[2048,256]{1,0:T(8,128)(2,1)S(1)}, bf16[2048,256]{1,0:T(8,128)(2,1)S(1)}, u32[]{:S(2)}, u32[]{:S(2)}) collective-permute-start(bf16[2048,256]{1,0:T(8,128)(2,1)S(1)} %shard_map.49), channel_id=1, source_target_pairs={{0,1},{1,0},{2,3},{3,2},{4,5},{5,4},{6,7},{7,6},{8,9},{9,8},{10,11... | collective-permute-start | bytes 3145736 | tf_op jit(solution)/shard_map/ppermute | solution.py:244
  89.8 9.2 %collective-permute-start.1 = (bf16[8,256,256]{2,1,0:T(8,128)(2,1)S(1)}, bf16[8,256,256]{2,1,0:T(8,128)(2,1)S(1)}, u32[]{:S(2)}, u32[]{:S(2)}) collective-permute-start(bf16[8,256,256]{2,1,0:T(8,128)(2,1)S(1)} %all_to_all.32.mine_ref), channel_id=1, source_target_pairs={{0,1},{1,0},{2,3},{3,2},{4,5},{5,4},{6,7},{7,6},{8,9},{9,8},{10,11... | collective-permute-start | bytes 3145736 | tf_op jit(solution)/shard_map/ppermute | solution.py:253
  106.8 22.6 %collective-permute-start.2 = (f32[48,1024]{1,0:T(8,128)S(1)}, f32[48,1024]{1,0:T(8,128)S(1)}, u32[]{:S(2)}, u32[]{:S(2)}) collective-permute-start(f32[48,1024]{1,0:T(8,128)S(1)} %get-tuple-element.5), channel_id=1, source_target_pairs={{0,0},{1,16},{16,1},{17,17},{2,2},{3,18},{18,3},{19,19},{4,4},{5,2... | collective-permute-start | bytes 589832 | tf_op jit(solution)/shard_map/ppermute | solution.py:255

commit v9 on v8

--- a/solution.py
+++ b/solution.py
@@ -10,7 +10,7 @@
 NAMES = ("x", "zh", "zl", "yl", "yh", "core")
 DP = ("x", "zh", "zl", "yl")
 TENSOR = ("yh", "core")
-PLANE = ("x", "yl")
+PLANE = ("yl", "x")
 DEPTH = ("zl", "zh")
 SPREAD = ("core", "zl", "yl", "x", "yh")
 F32 = jnp.float32
@@ -42,7 +42,7 @@
     mine = pl.multiple_of(lax.axis_index("zh") * rows, rows)
     start = pl.multiple_of(first + lax.axis_index("zh") * (4 * rows), rows)
     for index in range(n_tiles):
-        col, row = index // 2, index % 2
+        row, col = index // 4, index % 4
         here = pl.multiple_of((2 * row + core) * high, high)
         there = pl.multiple_of((2 * row + 1 - core) * high, high)
         grad[pl.ds(here, high), col * wide : (col + 1) * wide] = mine_ref[index]
@@ -235,7 +235,7 @@
     ]
     sent = jnp.stack(
         [
-            jnp.concatenate([halves[i % 2], up_grad[:, i // 2 * 256 : i // 2 * 256 + 256]], axis=0)
+            jnp.concatenate([halves[i // 4], up_grad[:, i % 4 * 256 : i % 4 * 256 + 256]], axis=0)
             for i in range(plane)
         ]
     )

time: 130 us -> 130 us (level)
  blocking collectives: 96.3 us -> 94.9 us
where the time goes in v9:
time: 130 us
  blocking collectives  94.9 us (73%)
  starting transfers between devices  18.7 us (14%)
  Pallas kernels  8.83 us (7%)
  waiting for transfers between devices  4.04 us (3%)
  local copies, waits for them, and re-layouts  1.35 us (1%)
    all_to_all x1, blocking collectives, per_device(): got = lax.all_to_all(sent, PLANE, 0, 0, tiled=True)  28.6 us
    all_to_all x1, blocking collectives, per_device(): lax.all_to_all(tile.reshape(depth, 64, 256), DEPTH, 0, 0, tiled=True)  22.9 us
    all_to_all x1, blocking collectives, per_device(): totals = lax.all_to_all(total, SPREAD, 0, 0, tiled=True)  17.9 us
    all_to_all x1, blocking collectives, per_device(): lax.all_to_all(jnp.broadcast_to(tile[None], (plane, 256, 256)), PLANE, 0,...  13.4 us
    all_to_all x1, blocking collectives, per_device(): tile = lax.all_to_all(pieces, 'zh', 0, 0, tiled=True).reshape(256, 256)  12.1 us
    pallas_call x1, Pallas kernels, roots(): pl.pallas_call(roots_kernel, out_shape=(jax.ShapeDtypeStruct((3 * rows, w...  7.8 us
    ppermute x1, starting transfers between devices, per_device(): other = lax.ppermute(mine, 'core', swap)  7.51 us
    ppermute x1, starting transfers between devices, per_device(): other = lax.ppermute(cut(got), 'core', swap)  7.06 us
  transfers between devices with their start and end apart: 3, of which 2 were waited for; matrix products, arithmetic and copies ran while one was open for 0% of the time, Pallas kernels for 0%

profile of v9, /device:TPU:1, one launch (start us, length us, event | category | flops | bytes accessed | tf_op | source)
XLA Modules:
  0.0 129.7 jit_solution(4429542400972112181)
XLA Ops:
  0.6 1.3 constant_dynamic-slice_fusion
  2.1 28.6 %all_to_all.29.got_ref = bf16[8,512,256]{2,1,0:T(8,128)(2,1)S(1)} all-to-all(bf16[8,512,256]{2,1,0:T(8,128)(2,1)S(1)} %fusion.7), channel_id=1, replica_groups=mesh['x'=4,'zh'=4,'zl'=2,'yl'=2,'yh'=4,'core'=2] {'yl','x'}, dimensions={0} | all-to-all | bytes 4194304 | tf_op jit(solution)/shard_map/all_to_all | solution.py:242
  30.7 0.1 shard_map.49
  30.8 7.1 %collective-permute-start = (bf16[2048,256]{1,0:T(8,128)(2,1)S(1)}, bf16[2048,256]{1,0:T(8,128)(2,1)S(1)}, u32[]{:S(2)}, u32[]{:S(2)}) collective-permute-start(bf16[2048,256]{1,0:T(8,128)(2,1)S(1)} %shard_map.49), channel_id=1, source_target_pairs={{0,1},{1,0},{2,3},{3,2},{4,5},{5,4},{6,7},{7,6},{8,9},{9,8},{10,11... | collective-permute-start | bytes 3145736 | tf_op jit(solution)/shard_map/ppermute | solution.py:244
  37.8 0.5 shard_map.50.mine_ref
  38.3 1.8 %collective-permute-done.other_ref = bf16[2048,256]{1,0:T(8,128)(2,1)S(1)} collective-permute-done((bf16[2048,256]{1,0:T(8,128)(2,1)S(1)}, bf16[2048,256]{1,0:T(8,128)(2,1)S(1)}, u32[]{:S(2)}, u32[]{:S(2)}) %collective-permute-start) | collective-permute-done | bytes 1048608 | tf_op jit(solution)/shard_map/ppermute | solution.py:244
  40.1 0.5 shard_map.51
  40.6 22.9 %all_to_all.30 = f32[8,64,256]{2,1,0:T(8,128)S(1)} all-to-all(f32[8,64,256]{2,1,0:T(8,128)S(1)} %bitcast.40), channel_id=1, replica_groups=mesh['x'=4,'zh'=4,'zl'=2,'yl'=2,'yh'=4,'core'=2] {'zl','zh'}, dimensions={0} | all-to-all | bytes 1048576 | tf_op jit(solution)/shard_map/all_to_all | solution.py:246
  63.5 12.1 %all_to_all.31 = bf16[4,64,256]{2,1,0:T(8,128)(2,1)S(1)} all-to-all(bf16[4,64,256]{2,1,0:T(8,128)(2,1)S(1)} %broadcast_in_dim.16), channel_id=1, replica_groups=mesh['x'=4,'zh'=4,'zl'=2,'yl'=2,'yh'=4,'core'=2] {'zh'}, dimensions={0} | all-to-all | bytes 262144 | tf_op jit(solution)/shard_map/all_to_all | solution.py:249
  75.7 0.1 broadcast_in_dim.18
  75.7 13.4 %all_to_all.32.mine_ref = bf16[8,256,256]{2,1,0:T(8,128)(2,1)S(1)} all-to-all(bf16[8,256,256]{2,1,0:T(8,128)(2,1)S(1)} %broadcast_in_dim.18), channel_id=1, replica_groups=mesh['x'=4,'zh'=4,'zl'=2,'yl'=2,'yh'=4,'core'=2] {'yl','x'}, dimensions={0} | all-to-all | bytes 2097152 | tf_op jit(solution)/shard_map/all_to_all | solution.py:250
  89.1 7.5 %collective-permute-start.1 = (bf16[8,256,256]{2,1,0:T(8,128)(2,1)S(1)}, bf16[8,256,256]{2,1,0:T(8,128)(2,1)S(1)}, u32[]{:S(2)}, u32[]{:S(2)}) collective-permute-start(bf16[8,256,256]{2,1,0:T(8,128)(2,1)S(1)} %all_to_all.32.mine_ref), channel_id=1, source_target_pairs={{0,1},{1,0},{2,3},{3,2},{4,5},{5,4},{6,7},{7,6},{8,9},{9,8},{10,11... | collective-permute-start | bytes 3145736 | tf_op jit(solution)/shard_map/ppermute | solution.py:253
  96.7 2.3 %collective-permute-done.1.other_ref = bf16[8,256,256]{2,1,0:T(8,128)(2,1)S(1)} collective-permute-done((bf16[8,256,256]{2,1,0:T(8,128)(2,1)S(1)}, bf16[8,256,256]{2,1,0:T(8,128)(2,1)S(1)}, u32[]{:S(2)}, u32[]{:S(2)}) %collective-permute-start.1) | collective-permute-done | bytes 1048608 | tf_op jit(solution)/shard_map/ppermute | solution.py:253
  98.9 7.8 %shard_map.52 = (f32[48,1024]{1,0:T(8,128)S(1)}, f32[128,128]{1,0:T(8,128)S(1)}) custom-call(bf16[8,256,256]{2,1,0:T(8,128)(2,1)S(1)} %all_to_all.32.mine_ref, bf16[8,256,256]{2,1,0:T(8,128)(2,1)S(1)} %collective-permute-done.1.other_ref), custom_call_target="tpu_custom_call" | custom-call | tf_op jit(solution)/shard_map/pallas_call | solution.py:145
  106.7 4.2 %collective-permute-start.2 = (f32[48,1024]{1,0:T(8,128)S(1)}, f32[48,1024]{1,0:T(8,128)S(1)}, u32[]{:S(2)}, u32[]{:S(2)}) collective-permute-start(f32[48,1024]{1,0:T(8,128)S(1)} %get-tuple-element.5), channel_id=1, source_target_pairs={{0,0},{1,16},{16,1},{17,17},{2,2},{3,18},{18,3},{19,19},{4,4},{5,2... | collective-permute-start | bytes 589832 | tf_op jit(solution)/shard_map/ppermute | solution.py:255
  110.9 17.9 %all_to_all.33 = f32[128,1,128]{2,1,0:T(1,128)S(1)} all-to-all(f32[128,1,128]{2,1,0:T(1,128)S(1)} %bitcast.41), channel_id=1, replica_groups=mesh['x'=4,'zh'=4,'zl'=2,'yl'=2,'yh'=4,'core'=2] {'core','zl','yl','x','..., dimensions={0} | all-to-all | bytes 131072 | tf_op jit(solution)/shard_map/all_to_all | solution.py:256
  128.8 0.2 reduce_sum.19
  129.1 0.0 collective-permute-done.2
  129.1 0.7 slice_multiply_fusion
  (11 shorter events, 0.2 us)
Async XLA Ops:
  30.8 9.3 %collective-permute-start = (bf16[2048,256]{1,0:T(8,128)(2,1)S(1)}, bf16[2048,256]{1,0:T(8,128)(2,1)S(1)}, u32[]{:S(2)}, u32[]{:S(2)}) collective-permute-start(bf16[2048,256]{1,0:T(8,128)(2,1)S(1)} %shard_map.49), channel_id=1, source_target_pairs={{0,1},{1,0},{2,3},{3,2},{4,5},{5,4},{6,7},{7,6},{8,9},{9,8},{10,11... | collective-permute-start | bytes 3145736 | tf_op jit(solution)/shard_map/ppermute | solution.py:244
  89.1 9.8 %collective-permute-start.1 = (bf16[8,256,256]{2,1,0:T(8,128)(2,1)S(1)}, bf16[8,256,256]{2,1,0:T(8,128)(2,1)S(1)}, u32[]{:S(2)}, u32[]{:S(2)}) collective-permute-start(bf16[8,256,256]{2,1,0:T(8,128)(2,1)S(1)} %all_to_all.32.mine_ref), channel_id=1, source_target_pairs={{0,1},{1,0},{2,3},{3,2},{4,5},{5,4},{6,7},{7,6},{8,9},{9,8},{10,11... | collective-permute-start | bytes 3145736 | tf_op jit(solution)/shard_map/ppermute | solution.py:253
  106.7 22.3 %collective-permute-start.2 = (f32[48,1024]{1,0:T(8,128)S(1)}, f32[48,1024]{1,0:T(8,128)S(1)}, u32[]{:S(2)}, u32[]{:S(2)}) collective-permute-start(f32[48,1024]{1,0:T(8,128)S(1)} %get-tuple-element.5), channel_id=1, source_target_pairs={{0,0},{1,16},{16,1},{17,17},{2,2},{3,18},{18,3},{19,19},{4,4},{5,2... | collective-permute-start | bytes 589832 | tf_op jit(solution)/shard_map/ppermute | solution.py:255

commit v10 on v9

--- a/solution.py
+++ b/solution.py
@@ -53,6 +53,7 @@
         jnp.int32, (side, side), 1
     )
     squares = crossed = squared = jnp.zeros((side, side), F32)
+    squares_on = crossed_on = squared_on = squares
     diagonal, rounded = [], []
     for row in range(0, width, side):
         part = grad[row : row + side, :]
@@ -68,20 +69,20 @@
             if col > row:
                 stat[col : col + side, row : row + side] = tile_low.T
                 rest[col : col + side, row : row + side] = tile_rest.T
-                squares += 2.0 * (tile * tile)
+                squares += tile * tile
                 crossed += tile * back
                 squared += back * back
             else:
                 outside = jnp.where(on_diagonal, 0.0, back)
                 damped = jnp.where(on_diagonal, tile + DAMPING, tile)
-                squares += damped * damped
-                crossed += 0.5 * (tile * outside)
-                squared += 0.5 * (outside * outside)
+                squares_on += damped * damped
+                crossed_on += tile * outside
+                squared_on += outside * outside
                 diagonal.append(jnp.sum(jnp.where(on_diagonal, tile, 0.0), axis=0, keepdims=True))
                 rounded.append(jnp.sum(jnp.where(on_diagonal, back, 0.0), axis=0, keepdims=True))
-    inverse = lax.rsqrt(jnp.full((1, 1), jnp.sum(squares), F32))
-    above = jnp.full((1, 1), jnp.sum(crossed), F32)
-    below = jnp.full((1, 1), jnp.sum(squared), F32)
+    inverse = lax.rsqrt(jnp.full((1, 1), jnp.sum(2.0 * squares + squares_on), F32))
+    above = jnp.full((1, 1), jnp.sum(2.0 * crossed + crossed_on), F32)
+    below = jnp.full((1, 1), jnp.sum(2.0 * squared + squared_on), F32)
     gain = jnp.where(below > 0.0, above / jnp.where(below > 0.0, below, 1.0), 1.0)
     delta = DAMPING * inverse
     tau = 1.25 - 0.25 * delta

time: 130 us -> 130 us (level)
  no operation moved by 1% of the time
where the time goes in v10:
time: 130 us
  blocking collectives  94.9 us (73%)
  starting transfers between devices  18.7 us (14%)
  Pallas kernels  8.7 us (7%)
  waiting for transfers between devices  4.04 us (3%)
  local copies, waits for them, and re-layouts  1.35 us (1%)
    all_to_all x1, blocking collectives, per_device(): got = lax.all_to_all(sent, PLANE, 0, 0, tiled=True)  28.6 us
    all_to_all x1, blocking collectives, per_device(): lax.all_to_all(tile.reshape(depth, 64, 256), DEPTH, 0, 0, tiled=True)  22.9 us
    all_to_all x1, blocking collectives, per_device(): totals = lax.all_to_all(total, SPREAD, 0, 0, tiled=True)  17.9 us
    all_to_all x1, blocking collectives, per_device(): lax.all_to_all(jnp.broadcast_to(tile[None], (plane, 256, 256)), PLANE, 0,...  13.4 us
    all_to_all x1, blocking collectives, per_device(): tile = lax.all_to_all(pieces, 'zh', 0, 0, tiled=True).reshape(256, 256)  12.1 us
    pallas_call x1, Pallas kernels, roots(): pl.pallas_call(roots_kernel, out_shape=(jax.ShapeDtypeStruct((3 * rows, w...  7.68 us
    ppermute x1, starting transfers between devices, per_device(): other = lax.ppermute(mine, 'core', swap)  7.51 us
    ppermute x1, starting transfers between devices, per_device(): other = lax.ppermute(cut(got), 'core', swap)  7.06 us
  transfers between devices with their start and end apart: 3, of which 2 were waited for; matrix products, arithmetic and copies ran while one was open for 0% of the time, Pallas kernels for 0%

profile of v10, /device:TPU:1, one launch (start us, length us, event | category | flops | bytes accessed | tf_op | source)
XLA Modules:
  0.0 129.6 jit_solution(4293211263694257503)
XLA Ops:
  0.6 1.3 constant_dynamic-slice_fusion
  2.1 28.6 %all_to_all.29.got_ref = bf16[8,512,256]{2,1,0:T(8,128)(2,1)S(1)} all-to-all(bf16[8,512,256]{2,1,0:T(8,128)(2,1)S(1)} %fusion.7), channel_id=1, replica_groups=mesh['x'=4,'zh'=4,'zl'=2,'yl'=2,'yh'=4,'core'=2] {'yl','x'}, dimensions={0} | all-to-all | bytes 4194304 | tf_op jit(solution)/shard_map/all_to_all | solution.py:243
  30.7 0.1 shard_map.49
  30.8 7.1 %collective-permute-start = (bf16[2048,256]{1,0:T(8,128)(2,1)S(1)}, bf16[2048,256]{1,0:T(8,128)(2,1)S(1)}, u32[]{:S(2)}, u32[]{:S(2)}) collective-permute-start(bf16[2048,256]{1,0:T(8,128)(2,1)S(1)} %shard_map.49), channel_id=1, source_target_pairs={{0,1},{1,0},{2,3},{3,2},{4,5},{5,4},{6,7},{7,6},{8,9},{9,8},{10,11... | collective-permute-start | bytes 3145736 | tf_op jit(solution)/shard_map/ppermute | solution.py:245
  37.8 0.5 shard_map.50.mine_ref
  38.3 1.8 %collective-permute-done.other_ref = bf16[2048,256]{1,0:T(8,128)(2,1)S(1)} collective-permute-done((bf16[2048,256]{1,0:T(8,128)(2,1)S(1)}, bf16[2048,256]{1,0:T(8,128)(2,1)S(1)}, u32[]{:S(2)}, u32[]{:S(2)}) %collective-permute-start) | collective-permute-done | bytes 1048608 | tf_op jit(solution)/shard_map/ppermute | solution.py:245
  40.1 0.5 shard_map.51
  40.6 22.9 %all_to_all.30 = f32[8,64,256]{2,1,0:T(8,128)S(1)} all-to-all(f32[8,64,256]{2,1,0:T(8,128)S(1)} %bitcast.40), channel_id=1, replica_groups=mesh['x'=4,'zh'=4,'zl'=2,'yl'=2,'yh'=4,'core'=2] {'zl','zh'}, dimensions={0} | all-to-all | bytes 1048576 | tf_op jit(solution)/shard_map/all_to_all | solution.py:247
  63.5 12.1 %all_to_all.31 = bf16[4,64,256]{2,1,0:T(8,128)(2,1)S(1)} all-to-all(bf16[4,64,256]{2,1,0:T(8,128)(2,1)S(1)} %broadcast_in_dim.16), channel_id=1, replica_groups=mesh['x'=4,'zh'=4,'zl'=2,'yl'=2,'yh'=4,'core'=2] {'zh'}, dimensions={0} | all-to-all | bytes 262144 | tf_op jit(solution)/shard_map/all_to_all | solution.py:250
  75.7 0.1 broadcast_in_dim.18
  75.7 13.4 %all_to_all.32.mine_ref = bf16[8,256,256]{2,1,0:T(8,128)(2,1)S(1)} all-to-all(bf16[8,256,256]{2,1,0:T(8,128)(2,1)S(1)} %broadcast_in_dim.18), channel_id=1, replica_groups=mesh['x'=4,'zh'=4,'zl'=2,'yl'=2,'yh'=4,'core'=2] {'yl','x'}, dimensions={0} | all-to-all | bytes 2097152 | tf_op jit(solution)/shard_map/all_to_all | solution.py:251
  89.1 7.5 %collective-permute-start.1 = (bf16[8,256,256]{2,1,0:T(8,128)(2,1)S(1)}, bf16[8,256,256]{2,1,0:T(8,128)(2,1)S(1)}, u32[]{:S(2)}, u32[]{:S(2)}) collective-permute-start(bf16[8,256,256]{2,1,0:T(8,128)(2,1)S(1)} %all_to_all.32.mine_ref), channel_id=1, source_target_pairs={{0,1},{1,0},{2,3},{3,2},{4,5},{5,4},{6,7},{7,6},{8,9},{9,8},{10,11... | collective-permute-start | bytes 3145736 | tf_op jit(solution)/shard_map/ppermute | solution.py:254
  96.7 2.3 %collective-permute-done.1.other_ref = bf16[8,256,256]{2,1,0:T(8,128)(2,1)S(1)} collective-permute-done((bf16[8,256,256]{2,1,0:T(8,128)(2,1)S(1)}, bf16[8,256,256]{2,1,0:T(8,128)(2,1)S(1)}, u32[]{:S(2)}, u32[]{:S(2)}) %collective-permute-start.1) | collective-permute-done | bytes 1048608 | tf_op jit(solution)/shard_map/ppermute | solution.py:254
  98.9 7.7 %shard_map.52 = (f32[48,1024]{1,0:T(8,128)S(1)}, f32[128,128]{1,0:T(8,128)S(1)}) custom-call(bf16[8,256,256]{2,1,0:T(8,128)(2,1)S(1)} %all_to_all.32.mine_ref, bf16[8,256,256]{2,1,0:T(8,128)(2,1)S(1)} %collective-permute-done.1.other_ref), custom_call_target="tpu_custom_call" | custom-call | tf_op jit(solution)/shard_map/pallas_call | solution.py:146
  106.6 4.2 %collective-permute-start.2 = (f32[48,1024]{1,0:T(8,128)S(1)}, f32[48,1024]{1,0:T(8,128)S(1)}, u32[]{:S(2)}, u32[]{:S(2)}) collective-permute-start(f32[48,1024]{1,0:T(8,128)S(1)} %get-tuple-element.5), channel_id=1, source_target_pairs={{0,0},{1,16},{16,1},{17,17},{2,2},{3,18},{18,3},{19,19},{4,4},{5,2... | collective-permute-start | bytes 589832 | tf_op jit(solution)/shard_map/ppermute | solution.py:256
  110.8 17.9 %all_to_all.33 = f32[128,1,128]{2,1,0:T(1,128)S(1)} all-to-all(f32[128,1,128]{2,1,0:T(1,128)S(1)} %bitcast.41), channel_id=1, replica_groups=mesh['x'=4,'zh'=4,'zl'=2,'yl'=2,'yh'=4,'core'=2] {'core','zl','yl','x','..., dimensions={0} | all-to-all | bytes 131072 | tf_op jit(solution)/shard_map/all_to_all | solution.py:257
  128.7 0.2 reduce_sum.19
  128.9 0.0 collective-permute-done.2
  128.9 0.7 slice_multiply_fusion
  (11 shorter events, 0.2 us)
Async XLA Ops:
  30.8 9.3 %collective-permute-start = (bf16[2048,256]{1,0:T(8,128)(2,1)S(1)}, bf16[2048,256]{1,0:T(8,128)(2,1)S(1)}, u32[]{:S(2)}, u32[]{:S(2)}) collective-permute-start(bf16[2048,256]{1,0:T(8,128)(2,1)S(1)} %shard_map.49), channel_id=1, source_target_pairs={{0,1},{1,0},{2,3},{3,2},{4,5},{5,4},{6,7},{7,6},{8,9},{9,8},{10,11... | collective-permute-start | bytes 3145736 | tf_op jit(solution)/shard_map/ppermute | solution.py:245
  89.1 9.8 %collective-permute-start.1 = (bf16[8,256,256]{2,1,0:T(8,128)(2,1)S(1)}, bf16[8,256,256]{2,1,0:T(8,128)(2,1)S(1)}, u32[]{:S(2)}, u32[]{:S(2)}) collective-permute-start(bf16[8,256,256]{2,1,0:T(8,128)(2,1)S(1)} %all_to_all.32.mine_ref), channel_id=1, source_target_pairs={{0,1},{1,0},{2,3},{3,2},{4,5},{5,4},{6,7},{7,6},{8,9},{9,8},{10,11... | collective-permute-start | bytes 3145736 | tf_op jit(solution)/shard_map/ppermute | solution.py:254
  106.6 22.3 %collective-permute-start.2 = (f32[48,1024]{1,0:T(8,128)S(1)}, f32[48,1024]{1,0:T(8,128)S(1)}, u32[]{:S(2)}, u32[]{:S(2)}) collective-permute-start(f32[48,1024]{1,0:T(8,128)S(1)} %get-tuple-element.5), channel_id=1, source_target_pairs={{0,0},{1,16},{16,1},{17,17},{2,2},{3,18},{18,3},{19,19},{4,4},{5,2... | collective-permute-start | bytes 589832 | tf_op jit(solution)/shard_map/ppermute | solution.py:256
